TPU v7x, 256 devices: a whole 4x4x8 slice. The times are simulated.
256 devices in a mesh: ctx: 32 (over z, y_lo, core), exp: 8 (over x, y_hi).
Axes of the slice: x: 4, y: 4 (y_hi: 2, y_lo: 2; y = y_hi * 2 + y_lo), z: 8, core: 2. Of those that a mesh axis runs over, the one named last changes fastest.
Arguments:
- hidden_in: bfloat16 [512, 6144], P(None, 'ctx'), may hold values from -4 to 4
- queries: bfloat16 [512, 6144], P(None, 'exp'), may hold values from -48 to 48
- keys: bfloat16 [16384, 1024], P('ctx', 'exp'), may hold values from -24 to 24
- values: bfloat16 [16384, 1024], P('ctx', 'exp'), may hold values from -6 to 6
- out_weight: bfloat16 [6144, 6144], P('exp', 'ctx'), may hold values from -0.078125 to 0.078125
- norm_gain: float32 [6144], replicated, may hold values from 0.25 to 1.75
- expert_gate: bfloat16 [8, 6144, 8192], P('exp', None, 'ctx'), may hold values from -0.078125 to 0.078125
- expert_up: bfloat16 [8, 6144, 8192], P('exp', None, 'ctx'), may hold values from -0.078125 to 0.078125
- expert_down: bfloat16 [8, 8192, 6144], P('exp', 'ctx'), may hold values from -0.125 to 0.125
- expert_ids: int32 [512, 2], replicated, may hold values from 0 to 7, all different within a row; in each aligned block of 512 rows (0 to 511, 512 to 1023, ...) at most 256 rows name the same one
- route_weights: float32 [512, 2], replicated, may hold values from 0.2 to 1
Outputs:
- mixed: bfloat16 [512, 6144], P('exp', 'ctx')
Inputs may be any that keep to these rules, and one draw needn't show every extreme that they name: `expert_ids`: the two experts of a token differ; no expert is named by more than 256 tokens of the slab, a bound that some block reaches.
All inputs are finite; a program needn't handle non-finite values.
Results may differ from a plain program's by a relative error of at most 0.03.
Values may be sent and summed in bfloat16 or wider, within the bound.
A program may use at most 192 MiB of HBM per device.

v0:
```python
import math

import jax
import jax.numpy as jnp
from jax import lax
from jax.sharding import PartitionSpec as P

D = 6144
HD = 128


def from_behind(value, axis, steps):
    count = lax.axis_size(axis)
    pairs = [(source, (source + steps) % count) for source in range(count)]
    return lax.ppermute(value, axis, pairs)


def block_scores(query_block, first_row, key_block, value_block, first_key, context_len, slab_len):
    row_count = query_block.shape[0]
    key_count = key_block.shape[0]
    scores = jnp.einsum(
        "qhd,kd->qhk", query_block, key_block, preferred_element_type=jnp.float32
    ) * (1.0 / math.sqrt(HD))
    query_pos = context_len - slab_len + first_row + jnp.arange(row_count, dtype=jnp.int32)
    key_pos = first_key + jnp.arange(key_count, dtype=jnp.int32)
    visible = key_pos[None, :] <= query_pos[:, None]
    scores = jnp.where(visible[:, None, :], scores, -1e30)
    peak = jnp.max(scores, axis=-1)
    weights = jnp.exp(scores - peak[..., None])
    totals = jnp.sum(weights, axis=-1)
    numer = jnp.einsum(
        "qhk,kd->qhd", weights.astype(jnp.bfloat16), value_block, preferred_element_type=jnp.float32
    )
    return (peak, totals, numer)


def merge_softmax(earlier, later):
    peak = jnp.maximum(earlier[0], later[0])
    first_factor = jnp.exp(earlier[0] - peak)
    second_factor = jnp.exp(later[0] - peak)
    totals = earlier[1] * first_factor + later[1] * second_factor
    numer = earlier[2] * first_factor[..., None] + later[2] * second_factor[..., None]
    return (peak, totals, numer)


def local(
    hidden_in,
    queries,
    keys,
    values,
    out_weight,
    norm_gain,
    expert_gate,
    expert_up,
    expert_down,
    expert_ids,
    route_weights,
):
    ctx_count = lax.axis_size("ctx")
    exp_count = lax.axis_size("exp")
    ctx_rank = lax.axis_index("ctx")
    exp_rank = lax.axis_index("exp")
    block_len = keys.shape[0]
    context_len = block_len * ctx_count
    slab_len = queries.shape[0]
    group_size = queries.shape[1] // HD
    col_width = hidden_in.shape[1]
    top_count = expert_ids.shape[1]
    capacity = min(slab_len, 2 * slab_len * top_count // exp_count)
    queries_all = queries.reshape(slab_len, group_size, HD)
    row_count = slab_len // ctx_count
    first_row = ctx_rank * row_count
    query_block = lax.dynamic_slice_in_dim(queries_all, first_row, row_count, 0)
    opening = block_scores(
        query_block, first_row, keys, values, ctx_rank * block_len, context_len, slab_len
    )

    def visit(turn_index, carried):
        state, cache_pair = carried
        cache_pair = from_behind(cache_pair, "ctx", 1)
        source = (ctx_rank - turn_index) % ctx_count
        fresh = block_scores(
            query_block,
            first_row,
            cache_pair[0],
            cache_pair[1],
            source * block_len,
            context_len,
            slab_len,
        )
        return (merge_softmax(state, fresh), cache_pair)

    final_state, _ = lax.fori_loop(1, ctx_count, visit, (opening, jnp.stack([keys, values])))
    own_rows = (
        (final_state[2] / final_state[1][..., None])
        .astype(jnp.bfloat16)
        .reshape(row_count, group_size * HD)
    )
    attended = lax.all_gather(own_rows, "ctx", axis=0, tiled=True)
    flat_ids = expert_ids.reshape(-1)
    one_hot = (flat_ids[:, None] == jnp.arange(exp_count, dtype=jnp.int32)[None, :]).astype(
        jnp.int32
    )
    earlier_count = jnp.cumsum(one_hot, axis=0) - one_hot
    slot_flat = jnp.sum(earlier_count * one_hot, axis=1)
    pair_token = jnp.arange(slab_len * top_count, dtype=jnp.int32) // top_count
    slot_token = (
        jnp.full((exp_count * capacity,), slab_len, jnp.int32)
        .at[flat_ids * capacity + slot_flat]
        .set(pair_token)
    )
    projected = jnp.dot(attended, out_weight, preferred_element_type=jnp.float32)
    projected_pad = jnp.concatenate([projected, jnp.zeros((1, col_width), jnp.float32)], axis=0)
    slot_attention = lax.psum_scatter(
        jnp.take(projected_pad, slot_token, axis=0).astype(jnp.bfloat16),
        "exp",
        scatter_dimension=0,
        tiled=True,
    ).astype(jnp.float32)
    my_tokens = lax.dynamic_slice_in_dim(slot_token, exp_rank * capacity, capacity, 0)
    hidden_pad = jnp.concatenate([hidden_in, jnp.zeros((1, col_width), jnp.bfloat16)], axis=0)
    slot_stream = (
        jnp.take(hidden_pad, my_tokens, axis=0).astype(jnp.float32) + slot_attention
    ).astype(jnp.bfloat16)
    gate_w = expert_gate[0]
    up_w = expert_up[0]
    down_w = expert_down[0]
    seg_full = lax.all_gather(slot_stream, "ctx", axis=1, tiled=True).astype(jnp.float32)
    scaled = (seg_full * norm_gain).astype(jnp.bfloat16)
    gate_acc = jnp.dot(scaled, gate_w, preferred_element_type=jnp.float32)
    up_acc = jnp.dot(scaled, up_w, preferred_element_type=jnp.float32)
    squares = jnp.sum(seg_full * seg_full, axis=1)
    gate_acc, up_acc, squares = (gate_acc, up_acc, squares)
    inverse_rms = lax.rsqrt(squares / D + 1e-05)
    hidden = (
        jax.nn.silu(gate_acc * inverse_rms[:, None]) * (up_acc * inverse_rms[:, None])
    ).astype(jnp.bfloat16)
    slot_pairs = slot_flat.reshape(slab_len, top_count)
    owned = expert_ids == exp_rank
    slot_index = jnp.where(owned, slot_pairs, capacity)
    stream_pad = jnp.concatenate([slot_stream, jnp.zeros((1, col_width), jnp.bfloat16)], axis=0)
    residual = jnp.take(stream_pad, slot_index[:, 0], axis=0).astype(jnp.float32)
    partial_out = jnp.dot(hidden, down_w, preferred_element_type=jnp.float32)
    col_blocks = partial_out.reshape(capacity, ctx_count, col_width).transpose(1, 0, 2)
    col_blocks = jnp.concatenate(
        [col_blocks, jnp.zeros((ctx_count, 1, col_width), jnp.float32)], axis=1
    )
    token_terms = jnp.zeros((ctx_count, slab_len, col_width), jnp.float32)
    for choice_slot in range(top_count):
        picked = jnp.take(col_blocks, slot_index[:, choice_slot], axis=1)
        token_terms = token_terms + route_weights[None, :, choice_slot, None] * picked
    own_block = (jnp.arange(ctx_count, dtype=jnp.int32) == ctx_rank).astype(jnp.float32)
    token_terms = token_terms + own_block[:, None, None] * residual[None]
    mixed = lax.psum_scatter(
        token_terms.reshape(ctx_count * slab_len, col_width),
        ("ctx", "exp"),
        scatter_dimension=0,
        tiled=True,
    )
    return mixed.astype(jnp.bfloat16)


def solution(mesh):
    placed = (
        P(None, "ctx"),
        P(None, "exp"),
        P("ctx", "exp"),
        P("ctx", "exp"),
        P("exp", "ctx"),
        P(),
        P("exp", None, "ctx"),
        P("exp", None, "ctx"),
        P("exp", "ctx", None),
        P(),
        P(),
    )
    return jax.shard_map(
        local, mesh=mesh, in_specs=placed, out_specs=P("exp", "ctx"), check_vma=False
    )
```

profile of v0, /device:TPU:1, one launch (start us, length us, event | category | flops | bytes accessed | tf_op | source)
XLA Modules:
  0.0 1933.3 jit_solution(17441173055722897555)
XLA Ops:
  24.3 294.9 %while.21 = (s32[]{:T(128)}, f32[16,6]{0,1:T(8,128)S(1)}, f32[16,6]{0,1:T(8,128)S(1)}, f32[16,6,128]{2,0,1:T(8,128)S(1)}, bf16[2,512,128]{2,1,0:T(8,128)(2,1)}, ...) while((s32[]{:T(128)}, f32[16,6]{0,1:T(8,128)S(1)}, ...), condition=%wide.region_9.10_spmd, body=%wide.region_6.9_spmd.sunk | while | flops 25555872 | bytes 2585138 | solution.py:93
  50.3 8.0 collective-permute-done
  59.9 8.0 collective-permute-done
  69.5 8.0 collective-permute-done
  79.1 8.0 collective-permute-done
  88.7 8.0 collective-permute-done
  98.3 8.0 collective-permute-done
  108.0 8.0 collective-permute-done
  184.8 8.0 collective-permute-done
  194.4 8.0 collective-permute-done
  204.0 8.0 collective-permute-done
  213.6 8.0 collective-permute-done
  319.2 39.4 %all_gather.6 = bf16[512,768]{1,0:T(8,128)(2,1)S(1)} all-gather(bf16[16,768]{1,0:T(8,128)(2,1)S(1)} %copy_bitcast_fusion), channel_id=1, replica_groups=mesh['ctx'=32,'exp'=8] {'ctx'}, dimensions={0}, use_global_device_ids=true | all-gather | bytes 811008 | tf_op jit(solution)/shard_map/all_gather | solution.py:99
  360.0 9.0 gather_fusion.1
  375.4 71.8 %reduce-scatter.5.cloned.1.call-done = bf16[256,192]{1,0:T(8,128)(2,1)} async-done(((bf16[2048,192]{1,0:T(8,128)(2,1)}), bf16[256,192]{1,0:T(8,128)(2,1)}) %reduce-scatter.5.cloned.1.call-update) | async-done | bytes 98320 | tf_op jit(solution)/shard_map/reduce_scatter | solution.py:114
  460.9 55.8 %all-gather.2.cloned.1.call-done = bf16[256,6144]{0,1:T(8,128)(2,1)} async-done(((bf16[256,192]{0,1:T(8,128)(2,1)}), bf16[256,6144]{0,1:T(8,128)(2,1)}) %all-gather.2.cloned.1.call-update) | async-done | bytes 3145744 | tf_op jit(solution)/shard_map/all_gather | solution.py:128
  524.2 10.4 convolution_bitcast_fusion
  534.6 9.4 copy.83
  544.0 8.4 concatenate.14.clone
  552.4 23.5 %gather_fusion.3 = f32[512,32,192]{2,1,0:T(8,128)} fusion(f32[32,257,192]{2,0,1:T(8,128)} %concatenate.14.clone, s32[1024]{0:T(1024)S(1)} %pad_clamp_fusion.2), kind=kCustom, calls=%fused_computation.clone | custom fusion | bytes 25167872 | tf_op jit(solution)/shard_map/jit(_take)/gather | solution.py:150
  575.9 23.6 %gather_fusion.4 = f32[512,32,192]{2,1,0:T(8,128)} fusion(f32[32,257,192]{2,0,1:T(8,128)} %concatenate.14.clone, s32[1024]{0:T(1024)S(1)} %pad_clamp_fusion.1), kind=kCustom, calls=%fused_computation.1.clone | custom fusion | bytes 25167872 | tf_op jit(solution)/shard_map/jit(_take)/gather | solution.py:150
  599.6 14.7 fusion.7
  614.3 19.5 %copy.79 = f32[32,512,192]{2,1,0:T(8,128)} copy(f32[32,512,192]{2,0,1:T(8,128)S(1)} %fusion.7) | data formatting | bytes 25165824
  633.8 1291.2 %reduce-scatter.7.cloned.1.call-done = f32[64,192]{1,0:T(8,128)} async-done(((f32[16384,192]{1,0:T(8,128)}), f32[64,192]{1,0:T(8,128)}) %reduce-scatter.7.cloned.1.call-update) | async-done | bytes 49168 | tf_op jit(solution)/shard_map/reduce_scatter | solution.py:154
  (381 shorter events, 253.0 us)
Async XLA Ops:
  6.5 440.6 %reduce-scatter.5.cloned.1.call-start = ((), (), s32[]{:S(2)}) async-start(), calls=%async_computation.2 | async-start | bytes 1179648 | tf_op jit(solution)/shard_map/reduce_scatter | solution.py:114
  40.5 8.2 collective-permute-start
  50.1 8.2 collective-permute-start
  59.7 8.2 collective-permute-start
  69.3 8.2 collective-permute-start
  78.9 8.2 collective-permute-start
  88.5 8.2 collective-permute-start
  98.1 8.2 collective-permute-start
  107.7 8.2 collective-permute-start
  117.4 8.2 collective-permute-start
  127.0 8.2 collective-permute-start
  184.6 8.2 collective-permute-start
  194.2 8.2 collective-permute-start
  203.8 8.2 collective-permute-start
  213.4 8.2 collective-permute-start
  223.0 8.2 collective-permute-start
  232.7 8.2 collective-permute-start
  242.3 8.2 collective-permute-start
  251.9 8.2 collective-permute-start
  261.5 8.2 collective-permute-start
  271.1 8.2 collective-permute-start
  280.7 8.2 collective-permute-start
  371.3 145.4 %all-gather.2.cloned.1.call-start = ((), (), s32[]{:S(2)}) async-start(), calls=%async_computation.3 | async-start | bytes 3244032 | tf_op jit(solution)/shard_map/all_gather | solution.py:128
  448.9 1476.1 %reduce-scatter.7.cloned.1.call-start = ((), (), s32[]{:S(2)}) async-start(), calls=%async_computation.4 | async-start | bytes 16842752 | tf_op jit(solution)/shard_map/reduce_scatter | solution.py:154
  (19 other events, 2094.5 us)
Sparse Core Ops, SparseCore 0:
  371.4 75.6 reduce-scatter.4
  449.2 67.4 all-gather.1
  633.9 1291.0 reduce-scatter.6
where the time goes:
time: 1950 us; the launch traced here: 1930 us
  waiting for transfers between devices  1660 us (85%)
  local copies, waits for them, and re-layouts  138 us (7%)
  other arithmetic  39.6 us (2%)
  blocking collectives  39.4 us (2%)
  matrix products  34.2 us (2%)
    reduce_scatter x1, waiting for transfers between devices, local(): lax.psum_scatter(token_terms.reshape(ctx_count * slab_len, col_width), ('...  1290 us
    ppermute x31, waiting for transfers between devices, from_behind(): return lax.ppermute(value, axis, pairs)  238 us
    reduce_scatter x1, waiting for transfers between devices, local(): lax.psum_scatter(jnp.take(projected_pad, slot_token, axis=0).astype(jnp.b...  71.8 us
    all_gather x1, waiting for transfers between devices, local(): lax.all_gather(slot_stream, 'ctx', axis=1, tiled=True).astype(jnp.float32)  55.8 us
    gather x2, local copies, waits for them, and re-layouts, local(): picked = jnp.take(col_blocks, slot_index[:, choice_slot], axis=1)  47 us
    unnamed x26, local copies, waits for them, and re-layouts  39.8 us
    all_gather x1, blocking collectives, local(): attended = lax.all_gather(own_rows, 'ctx', axis=0, tiled=True)  39.4 us
  transfers between devices with their start and end apart: 34, of which 34 were waited for; matrix products, arithmetic and copies ran while one was open for 1% of the time, Pallas kernels for 0%

commit v1 on v0

v1 whole, which is shorter than its diff:
```python
import math

import jax
import jax.numpy as jnp
from jax import lax
from jax.experimental import pallas as pl
from jax.experimental.pallas import tpu as pltpu
from jax.sharding import PartitionSpec as P

F32 = jnp.float32
BF16 = jnp.bfloat16
MESH = pl.DeviceIdType.MESH

HD = 128
D = 6144
Q = 512
CONTEXT = 16384
CHIPS = 16
ZN = 8
EN = 8
HEADS = 6
HALF = Q // 2
ROWS = HALF // CHIPS
PAIRS = ROWS * HEADS
BLK = 512
WIDE = 384
COLS = 192
SLOTS = 256
SH = SLOTS // 2
SQ = SH // 2
TOKB = HALF // EN
OUTR = Q // EN
FF = 256
MSG = PAIRS + 16
FAR = (8, 7, 9, 6, 10, 5, 11, 4, 12, 3, 13, 2, 14, 1, 15, 0)
GROUP = 4


def dot(a, b, dims=((1,), (0,))):
    return lax.dot_general(a, b, (dims, ((), ())), preferred_element_type=F32)


def iota(shape, dim):
    return lax.broadcasted_iota(jnp.int32, shape, dim)


def one_hot_columns(shape, shift, along):
    other = 1 - along
    return jnp.where(iota(shape, along) == iota(shape, other) + shift, 1.0, 0.0).astype(BF16)


def layer_kernel(
    ids_ref, rw_ref, gain_ref, q_hbm, k_hbm, v_hbm, hin_hbm, wout_hbm, gate_hbm, up_hbm, down_hbm,
    out_ref,
    q_s, k_s, v_s, h_s, w_s, wc_s, gate_s, up_s, down_s,
    num_s, got_s, own_s, att_s, ps_s, pr_s, own_p, st_s,
    xs_s, xr_s, x_s, acc_s, sq_s, part_s, ys_s, yr_s,
    h1rs, h1rr, h1ls, h1lr, h2rs, h2rr, h2ls, h2lr, f1s, f1r,
    o_s, os_s, or_s, rs_s, rr_s, ts_s, tr_s, town_s, tok_s,
    lsem, ssem, rsem, asem, arsem, bsem, brsem, psem, prsem, gsem, grsem, tsem, trsem,
    ysem, yrsem, xsem, xrsem, esem, ersem,
):
    c = lax.axis_index("ctx")
    e = lax.axis_index("exp")
    core = c % 2
    chip = c // 2
    y = chip % 2
    z = chip // 2
    sib = c + 1 - 2 * core
    ypeer = c + 2 - 4 * y
    right = ((z + 1) % ZN) * 4 + y * 2 + core
    left = ((z + ZN - 1) % ZN) * 4 + y * 2 + core

    def remote(src, dst, send, recv, ctx=None, ex=None):
        return pltpu.make_async_remote_copy(
            src_ref=src, dst_ref=dst, send_sem=send, recv_sem=recv,
            device_id=(c if ctx is None else ctx, e if ex is None else ex),
            device_id_type=MESH,
        )

    def arrived(ref, sem):
        pltpu.make_async_copy(ref, ref, sem).wait()

    sent = []

    def push(*args, **kw):
        copy = remote(*args, **kw)
        copy.start()
        sent.append(copy)

    barrier = pltpu.get_barrier_semaphore()

    def greet(ctx, ex):
        pl.semaphore_signal(barrier, inc=1, device_id=(ctx, ex), device_id_type=MESH)

    greet(sib, e)
    for d in range(1, CHIPS):
        greet(2 * ((chip + d) % CHIPS) + core, e)
    for d in range(1, EN):
        greet(c, (e + d) % EN)

    half_rows = pl.ds(pl.multiple_of(HALF * core, HALF), HALF)
    my_rows = pl.ds(pl.multiple_of(HALF * core + TOKB * e, TOKB), TOKB)
    sib_rows = pl.ds(pl.multiple_of(HALF * (1 - core) + TOKB * e, TOKB), TOKB)
    gate_h, up_h, down_h = gate_hbm.at[0], up_hbm.at[0], down_hbm.at[0]
    loads = [
        pltpu.make_async_copy(q_hbm.at[half_rows, :], q_s, lsem.at[0]),
        pltpu.make_async_copy(k_hbm, k_s.at[core], lsem.at[1]),
        pltpu.make_async_copy(v_hbm, v_s.at[core], lsem.at[2]),
        pltpu.make_async_copy(hin_hbm.at[my_rows, :], h_s.at[core], lsem.at[3]),
        pltpu.make_async_copy(wout_hbm, w_s.at[core], lsem.at[4]),
        pltpu.make_async_copy(gate_h, gate_s.at[core], lsem.at[5]),
        pltpu.make_async_copy(up_h, up_s.at[core], lsem.at[6]),
        pltpu.make_async_copy(down_h, down_s.at[core], lsem.at[7]),
    ]
    for load in loads[:5]:
        load.start()

    pl.semaphore_wait(barrier, 1 + (CHIPS - 1) + (EN - 1))

    push(k_hbm, k_s.at[core], ssem.at[0], rsem.at[0], ctx=sib)
    push(v_hbm, v_s.at[core], ssem.at[1], rsem.at[1], ctx=sib)
    push(hin_hbm.at[sib_rows, :], h_s.at[core], ssem.at[2], rsem.at[2], ctx=sib)
    push(wout_hbm, w_s.at[core], ssem.at[3], rsem.at[3], ctx=sib)
    for load in loads[5:]:
        load.start()
    push(gate_h, gate_s.at[core], ssem.at[4], rsem.at[4], ctx=sib)
    push(up_h, up_s.at[core], ssem.at[5], rsem.at[5], ctx=sib)
    push(down_h, down_s.at[core], ssem.at[6], rsem.at[6], ctx=sib)

    loads[0].wait()
    loads[1].wait()
    arrived(k_s.at[1 - core], rsem.at[0])
    loads[2].wait()
    arrived(v_s.at[1 - core], rsem.at[1])
    keys = k_s[...].reshape(2 * BLK, HD)
    vals = jnp.concatenate([v_s[...].reshape(2 * BLK, HD), jnp.ones((2 * BLK, HD), BF16)], axis=1)
    diag = iota((PAIRS, HD), 0) == iota((PAIRS, HD), 1)
    stat_row = iota((16, HD), 0)
    first_limit = CONTEXT - Q + HALF * core - 2 * BLK * chip
    for start in range(0, CHIPS, GROUP):
        owners = [(chip + d) % CHIPS for d in FAR[start : start + GROUP]]
        rows, limits = [], []
        for p in owners:
            at = pl.ds(pl.multiple_of(ROWS * p, ROWS), ROWS)
            for h in range(HEADS):
                rows.append(q_s[at, HD * h : HD * (h + 1)])
                limits.append(iota((ROWS, 1), 0) + (first_limit + ROWS * p))
        qg = jnp.concatenate(rows, axis=0)
        limit = jnp.concatenate(limits, axis=0)
        scores = dot(qg, keys, ((1,), (1,))) * (math.log2(math.e) / math.sqrt(HD))
        scores = jnp.where(iota(scores.shape, 1) <= limit, scores, -1e30)
        peak = jnp.max(scores, axis=1, keepdims=True)
        weights = jnp.exp2(scores - peak).astype(BF16)
        both = dot(weights, vals)
        total = both[:, HD:]
        numer = (both[:, :HD] / total).astype(BF16)
        peaks = jnp.broadcast_to(peak, total.shape)
        for g, p in enumerate(owners):
            part = slice(PAIRS * g, PAIRS * (g + 1))
            pk = jnp.sum(jnp.where(diag, peaks[part], 0.0), axis=0, keepdims=True)
            tt = jnp.sum(jnp.where(diag, total[part], 0.0), axis=0, keepdims=True)
            pk0 = pk.astype(BF16).astype(F32)
            pk1 = (pk - pk0).astype(BF16).astype(F32)
            pk2 = pk - pk0 - pk1
            tt0 = tt.astype(BF16).astype(F32)
            stats = jnp.where(stat_row == 0, pk0, 0.0)
            for at, term in ((1, pk1), (2, pk2), (3, tt0), (4, tt - tt0)):
                stats = jnp.where(stat_row == at, term, stats)
            d = FAR[start + g]
            if d:
                num_s[p, :PAIRS, :] = numer[part]
                num_s[p, PAIRS:, :] = stats.astype(BF16)
                push(num_s.at[p], got_s.at[chip], asem.at[d], arsem.at[chip], ctx=2 * p + core)
            else:
                own_s[:PAIRS, :] = numer[part]
                own_s[PAIRS:, :] = stats.astype(BF16)

    ids = ids_ref[...]
    owned = jnp.where((ids[0:1] == e) | (ids[1:2] == e), 1.0, 0.0)
    w_row = jnp.where(ids[0:1] == e, rw_ref[0:1, :], 0.0) + jnp.where(ids[1:2] == e, rw_ref[1:2, :], 0.0)
    before = jnp.where(iota((Q, Q), 0) < iota((Q, Q), 1), 1.0, 0.0).astype(BF16)
    rank = dot(jnp.broadcast_to(owned, (16, Q)).astype(BF16), before)[0:1]
    place = jnp.where(owned > 0.5, rank, -1.0)
    place_col = jnp.transpose(jnp.broadcast_to(place, (HD, Q)))
    for part in range(2):
        lane = (iota((Q, SH), 1) + SH * part).astype(F32)
        tok_s[:, SH * part : SH * (part + 1)] = jnp.where(place_col == lane, 1.0, 0.0).astype(BF16)
    slot_own = (iota((SH, Q), 0) + SH * core).astype(F32)
    w_slot = jnp.sum(jnp.where(place == slot_own, w_row, 0.0), axis=1, keepdims=True)

    spread = [one_hot_columns((COLS, WIDE), COLS * at, 1) for at in range(2)]
    loads[4].wait()
    arrived(w_s.at[1 - core], rsem.at[3])
    wc_s[...] = (dot(w_s[0], spread[0]) + dot(w_s[1], spread[1])).astype(BF16)

    peaks, totals, numers = [], [], []
    for d in range(CHIPS):
        source = (chip + d) % CHIPS
        block = own_s if d == 0 else got_s.at[source]
        if d:
            arrived(block, arsem.at[source])
        stats = block[PAIRS:, :].astype(F32)
        peaks.append(stats[0:1] + stats[1:2] + stats[2:3])
        totals.append(stats[3:4] + stats[4:5])
    top = peaks[0]
    for pk in peaks[1:]:
        top = jnp.maximum(top, pk)
    factors = [jnp.exp2(pk - top) * tt for pk, tt in zip(peaks, totals)]
    whole = factors[0]
    for f in factors[1:]:
        whole = whole + f
    inverse = 1.0 / jnp.maximum(whole, 1e-30)
    merged = jnp.zeros((PAIRS, HD), F32)
    for d in range(CHIPS):
        source = (chip + d) % CHIPS
        block = own_s if d == 0 else got_s.at[source]
        column = jnp.sum(jnp.where(diag, factors[d] * inverse, 0.0), axis=1, keepdims=True)
        merged = merged + column * block[:PAIRS, :].astype(F32)
    att_s[chip] = merged.astype(BF16)
    for d in FAR[:-1]:
        push(att_s.at[chip], att_s.at[chip], bsem.at[d], brsem.at[chip], ctx=2 * ((chip + d) % CHIPS) + core)
    for d in range(1, CHIPS):
        source = (chip + d) % CHIPS
        arrived(att_s.at[source], brsem.at[source])

    attended = jnp.concatenate(
        [att_s[:, ROWS * h : ROWS * (h + 1), :].reshape(HALF, HD) for h in range(HEADS)], axis=1
    )
    projected = dot(attended, wc_s[...])
    own_p[...] = projected
    ps_s[...] = projected.astype(BF16).reshape(EN, TOKB, WIDE)
    for d in range(1, EN):
        to = (e + d) % EN
        push(ps_s.at[to], pr_s.at[e], psem.at[d], prsem.at[e], ex=to)
    loads[3].wait()
    arrived(h_s.at[1 - core], rsem.at[2])
    stream = own_p[pl.ds(pl.multiple_of(TOKB * e, TOKB), TOKB), :]
    for d in range(1, EN):
        source = (e + d) % EN
        arrived(pr_s.at[source], prsem.at[source])
        stream = stream + pr_s[source].astype(F32)
    stream = stream + (dot(h_s[0], spread[0]) + dot(h_s[1], spread[1]))
    st_s[e] = stream.astype(BF16)
    for d in range(1, EN):
        to = (e + d) % EN
        push(st_s.at[e], st_s.at[e], gsem.at[d], grsem.at[e], ex=to)
    for d in range(1, EN):
        source = (e + d) % EN
        arrived(st_s.at[source], grsem.at[source])

    rows = st_s[...].reshape(HALF, WIDE)

    def slots_of(part):
        token = iota((SH, HALF), 1) + HALF * core
        pick = iota((SH, HALF), 0) + SH * part
        here = jnp.where(core == 0, place[:, :HALF], place[:, HALF:])
        hot = jnp.where(here == pick.astype(F32), 1.0, 0.0).astype(BF16)
        return dot(hot, rows)

    xs_s[...] = slots_of(1 - core).astype(BF16)
    push(xs_s, xr_s, ssem.at[7], rsem.at[7], ctx=sib)
    resid = st_s[pl.ds(2 * (e % 4), 2)].reshape(OUTR, WIDE)
    take_own = jnp.where(iota((WIDE, 256), 0) == iota((WIDE, 256), 1) + COLS * core, 1.0, 0.0)
    take_sib = jnp.where(iota((WIDE, 256), 0) == iota((WIDE, 256), 1) + COLS * (1 - core), 1.0, 0.0)
    valid = iota((WIDE, 256), 1) < COLS
    take_own = jnp.where(valid, take_own, 0.0).astype(BF16)
    take_sib = jnp.where(valid, take_sib, 0.0).astype(BF16)
    rs_s[...] = dot(resid, take_sib).astype(BF16)
    push(rs_s, rr_s, ssem.at[8], rsem.at[8], ctx=sib)
    resid_own = dot(resid, take_own)
    mine = slots_of(core)
    arrived(xr_s, rsem.at[7])
    x_s[z, y] = (mine + xr_s[...].astype(F32)).astype(BF16)

    top_half, low_half = pl.ds(0, SQ), pl.ds(SQ, SQ)
    zp = [(z + d) % ZN for d in range(ZN)]

    def near(d):
        return zp[d % ZN]

    def x_low(d, yy):
        return x_s.at[near(d), yy, low_half, :]

    def x_top(d):
        return x_s.at[near(d), :, top_half, :]

    own_top = x_s.at[z, y, top_half, :]
    push(own_top, own_top, xsem.at[0], xrsem.at[0], ctx=ypeer)
    push(x_low(0, y), x_low(0, y), xsem.at[8], xrsem.at[8], ctx=right)
    push(x_low(0, y), x_low(0, y), xsem.at[11], xrsem.at[11], ctx=left)
    push(x_low(0, y), x_low(0, y), tsem.at[0], trsem.at[z], ctx=ypeer)
    arrived(x_s.at[z, 1 - y, top_half, :], xrsem.at[0])
    push(x_top(0), x_top(0), xsem.at[1], xrsem.at[1], ctx=right)
    push(x_top(0), x_top(0), xsem.at[5], xrsem.at[5], ctx=left)

    loads[5].wait()
    loads[6].wait()
    arrived(gate_s.at[1 - core], rsem.at[4])
    arrived(up_s.at[1 - core], rsem.at[5])
    acc_s[...] = jnp.zeros_like(acc_s)
    sq_s[...] = jnp.zeros_like(sq_s)

    def project(d):
        zz = near(d)
        for yy in range(2):
            at = pl.ds(pl.multiple_of(WIDE * (2 * zz + yy), WIDE), WIDE)
            block = x_s[zz, yy].astype(F32)
            square = block * block
            sq_s[...] += square[:, :128] + square[:, 128:256] + square[:, 256:]
            scaled = (block * gain_ref[:, at]).astype(BF16)
            for kk in range(2):
                acc_s[0, kk] += dot(scaled, gate_s[kk, at, :])
                acc_s[1, kk] += dot(scaled, up_s[kk, at, :])

    def low_arrived(d):
        arrived(x_low(d, 1 - y), trsem.at[near(d)])

    for s in range(1, 5):
        if s <= 3:
            arrived(x_low(-s, y), xrsem.at[7 + s])
            if s < 3:
                push(x_low(-s, y), x_low(-s, y), xsem.at[8 + s], xrsem.at[8 + s], ctx=right)
            push(x_low(-s, y), x_low(-s, y), tsem.at[ZN - s], trsem.at[near(-s)], ctx=ypeer)
        arrived(x_low(s, y), xrsem.at[10 + s])
        if s < 4:
            push(x_low(s, y), x_low(s, y), xsem.at[11 + s], xrsem.at[11 + s], ctx=left)
        push(x_low(s, y), x_low(s, y), tsem.at[s], trsem.at[near(s)], ctx=ypeer)
        arrived(x_top(-s), xrsem.at[s])
        if s < 4:
            push(x_top(-s), x_top(-s), xsem.at[1 + s], xrsem.at[1 + s], ctx=right)
        if s <= 3:
            arrived(x_top(s), xrsem.at[4 + s])
            if s < 3:
                push(x_top(s), x_top(s), xsem.at[5 + s], xrsem.at[5 + s], ctx=left)
        if s == 1:
            low_arrived(0)
            project(0)
        else:
            low_arrived(s - 1)
            project(s - 1)
            low_arrived(1 - s)
            project(1 - s)
    low_arrived(4)
    project(4)

    inverse_rms = lax.rsqrt(jnp.sum(sq_s[...], axis=1, keepdims=True) / D + 1e-5)
    hidden = []
    for kk in range(2):
        gate_val = acc_s[0, kk] * inverse_rms
        up_val = acc_s[1, kk] * inverse_rms
        hidden.append((gate_val / (1.0 + jnp.exp(-gate_val)) * up_val).astype(BF16))
    loads[7].wait()
    arrived(down_s.at[1 - core], rsem.at[6])

    def expand(d):
        zz = near(d)
        for yy in range(2):
            at = pl.ds(pl.multiple_of(WIDE * (2 * zz + yy), WIDE), WIDE)
            part_s[zz, yy] = dot(hidden[0], down_s[0, :, at]) + dot(hidden[1], down_s[1, :, at])
        ys_s[zz] = part_s[zz, 1 - y, SQ:, :].astype(BF16)
        push(ys_s.at[zz], yr_s.at[zz], ysem.at[d % ZN], yrsem.at[zz], ctx=ypeer)

    def top_right(s):
        d = 4 - s
        value = part_s[near(d), :, :SQ, :]
        if s:
            arrived(h1rr.at[s - 1], esem_r(0, s - 1))
            value = value + h1rr[s - 1].astype(F32)
        h1rs[s] = value.astype(BF16)
        push(h1rs.at[s], h1rr.at[s], esem.at[s], ersem.at[s], ctx=right)

    def esem_r(kind, s):
        return ersem.at[4 * kind + s]

    def top_left(s):
        d = s - 3
        value = part_s[near(d), :, :SQ, :]
        if s:
            arrived(h1lr.at[s - 1], esem_r(1, s - 1))
            value = value + h1lr[s - 1].astype(F32)
        h1ls[s] = value.astype(BF16)
        push(h1ls.at[s], h1lr.at[s], esem.at[4 + s], esem_r(1, s), ctx=left)

    def low_value(d):
        arrived(yr_s.at[near(d)], yrsem.at[near(d)])
        return part_s[near(d), y, SQ:, :] + yr_s[near(d)].astype(F32)

    def low_right(s):
        value = low_value(3 - s)
        if s:
            arrived(h2rr.at[s - 1], esem_r(2, s - 1))
            value = value + h2rr[s - 1].astype(F32)
        h2rs[s] = value.astype(BF16)
        push(h2rs.at[s], h2rr.at[s], esem.at[8 + s], esem_r(2, s), ctx=right)

    def low_left(s):
        value = low_value(s - 4)
        if s:
            arrived(h2lr.at[s - 1], esem_r(3, s - 1))
            value = value + h2lr[s - 1].astype(F32)
        h2ls[s] = value.astype(BF16)
        push(h2ls.at[s], h2lr.at[s], esem.at[12 + s], esem_r(3, s), ctx=left)

    expand(4)
    top_right(0)
    expand(-3)
    top_left(0)
    expand(3)
    expand(-2)
    expand(2)
    expand(-1)
    expand(1)
    expand(0)
    low_left(0)
    low_right(0)
    for s in range(1, 4):
        top_right(s)
        if s < 3:
            top_left(s)
        low_left(s)
        if s < 3:
            low_right(s)
    arrived(h1rr.at[3], esem_r(0, 3))
    arrived(h1lr.at[2], esem_r(1, 2))
    ends = h1rr[3].astype(F32) + h1lr[2].astype(F32)
    top_sum = jnp.where(y == 0, ends[0], ends[1]) + part_s[z, y, :SQ, :]
    f1s[...] = (jnp.where(y == 0, ends[1], ends[0]) + part_s[z, 1 - y, :SQ, :]).astype(BF16)
    push(f1s, f1r, ssem.at[9], rsem.at[9], ctx=ypeer)
    low_sum = low_value(0)
    arrived(h2rr.at[2], esem_r(2, 2))
    arrived(h2lr.at[3], esem_r(3, 3))
    low_sum = low_sum + (h2rr[2].astype(F32) + h2lr[3].astype(F32))
    arrived(f1r, rsem.at[9])
    top_sum = top_sum + f1r[...].astype(F32)
    summed = (jnp.concatenate([top_sum, low_sum], axis=0) * w_slot).astype(BF16)

    os_s[...] = dot(summed, take_sib).astype(BF16)
    push(os_s, or_s, ssem.at[10], rsem.at[10], ctx=sib)
    own_cols = dot(summed, take_own).astype(BF16)
    arrived(or_s, rsem.at[10])
    o_s[core] = own_cols
    o_s[1 - core] = or_s[...]
    slots = o_s[...].reshape(SLOTS, 256)
    town_s[...] = dot(tok_s[...], slots).reshape(EN, OUTR, 256)
    ts_s[...] = town_s[...].astype(BF16)
    for d in range(1, EN):
        to = (e + d) % EN
        push(ts_s.at[to], tr_s.at[e], psem.at[EN + d], prsem.at[EN + e], ex=to)
    arrived(rr_s, rsem.at[8])
    mixed = town_s[e] + jnp.where(core == e // 4, resid_own, rr_s[...].astype(F32))
    for d in range(1, EN):
        source = (e + d) % EN
        arrived(tr_s.at[source], prsem.at[EN + source])
        mixed = mixed + tr_s[source].astype(F32)
    out_ref[...] = mixed[:, :COLS].astype(BF16)
    for copy in sent:
        copy.wait_send()


def local(hidden_in, queries, keys, values, out_weight, norm_gain, expert_gate, expert_up, expert_down, expert_ids, route_weights):
    vmem = pl.BlockSpec(memory_space=pltpu.VMEM)
    anywhere = pl.BlockSpec(memory_space=pl.ANY)
    dma = pltpu.SemaphoreType.DMA

    def buf(*shape, dtype=BF16):
        return pltpu.VMEM(shape, dtype)

    scratch = [
        buf(HALF, HEADS * HD), buf(2, BLK, HD), buf(2, BLK, HD), buf(2, TOKB, COLS),
        buf(2, HEADS * HD, COLS), buf(HEADS * HD, WIDE),
        buf(2, D, FF), buf(2, D, FF), buf(2, FF, D),
        buf(CHIPS, MSG, HD), buf(CHIPS, MSG, HD), buf(MSG, HD), buf(CHIPS, PAIRS, HD),
        buf(EN, TOKB, WIDE), buf(EN, TOKB, WIDE), buf(HALF, WIDE, dtype=F32), buf(EN, TOKB, WIDE),
        buf(SH, WIDE), buf(SH, WIDE), buf(ZN, 2, SH, WIDE),
        buf(2, 2, SH, FF, dtype=F32), buf(SH, 128, dtype=F32), buf(ZN, 2, SH, WIDE, dtype=F32),
        buf(ZN, SQ, WIDE), buf(ZN, SQ, WIDE),
        buf(4, 2, SQ, WIDE), buf(4, 2, SQ, WIDE), buf(3, 2, SQ, WIDE), buf(3, 2, SQ, WIDE),
        buf(3, SQ, WIDE), buf(3, SQ, WIDE), buf(4, SQ, WIDE), buf(4, SQ, WIDE),
        buf(SQ, WIDE), buf(SQ, WIDE),
        buf(2, SH, 256), buf(SH, 256), buf(SH, 256), buf(OUTR, 256), buf(OUTR, 256),
        buf(EN, OUTR, 256), buf(EN, OUTR, 256), buf(EN, OUTR, 256, dtype=F32), buf(Q, SLOTS),
        dma((8,)), dma((11,)), dma((11,)),
        dma((CHIPS,)), dma((CHIPS,)), dma((CHIPS,)), dma((CHIPS,)),
        dma((2 * EN,)), dma((2 * EN,)), dma((EN,)), dma((EN,)), dma((ZN,)), dma((ZN,)),
        dma((ZN,)), dma((ZN,)), dma((15,)), dma((15,)), dma((16,)), dma((16,)),
    ]
    return pl.pallas_call(
        layer_kernel,
        out_shape=jax.ShapeDtypeStruct((OUTR, COLS), BF16),
        in_specs=[vmem] * 3 + [anywhere] * 8,
        out_specs=vmem,
        scratch_shapes=scratch,
        compiler_params=pltpu.CompilerParams(
            collective_id=0, has_side_effects=True, vmem_limit_bytes=56 * 1024 * 1024
        ),
        cost_estimate=pl.CostEstimate(flops=3 * 10**9, bytes_accessed=12 * 10**6, transcendentals=2 * 10**6),
    )(
        expert_ids.T, route_weights.T, norm_gain.reshape(1, D), queries, keys, values, hidden_in,
        out_weight, expert_gate, expert_up, expert_down,
    )


def solution(mesh):
    placed = (
        P(None, "ctx"),
        P(None, "exp"),
        P("ctx", "exp"),
        P("ctx", "exp"),
        P("exp", "ctx"),
        P(),
        P("exp", None, "ctx"),
        P("exp", None, "ctx"),
        P("exp", "ctx", None),
        P(),
        P(),
    )
    return jax.shard_map(
        local, mesh=mesh, in_specs=placed, out_specs=P("exp", "ctx"), check_vma=False
    )
```

time: 1950 us -> 110 us (0.06)
  waiting for transfers between devices: 1660 us -> 0 us
  local copies, waits for them, and re-layouts: 138 us -> 5.01 us
  Pallas kernels: 0 us -> 105 us
  other arithmetic: 39.6 us -> 0 us
  blocking collectives: 39.4 us -> 0 us
  matrix products: 34.2 us -> 0 us
    reduce_scatter x2 -> x0, waiting for transfers between devices: 1360 us -> none  [the longest x1 1290 us: local(): lax.psum_scatter(token_terms.reshape(ctx_count * slab_len, col_width), ('...]
    ppermute x31 -> x0, waiting for transfers between devices: 238 us -> none  [from_behind(): return lax.ppermute(value, axis, pairs)]
    pallas_call x0 -> x1, Pallas kernels: none -> 105 us  [local(): pl.pallas_call(layer_kernel, out_shape=jax.ShapeDtypeStruct((OUTR, COLS),...]
    gather x5 -> x0, local copies, waits for them, and re-layouts: 59.1 us -> none  [the longest x2 47 us: local(): picked = jnp.take(col_blocks, slot_index[:, choice_slot], axis=1)]
    all_gather x1 -> x0, waiting for transfers between devices: 55.8 us -> none  [local(): lax.all_gather(slot_stream, 'ctx', axis=1, tiled=True).astype(jnp.float32)]
    all_gather x1 -> x0, blocking collectives: 39.4 us -> none  [local(): attended = lax.all_gather(own_rows, 'ctx', axis=0, tiled=True)]
    unnamed x26 -> x3, local copies, waits for them, and re-layouts: 39.8 us -> 5.01 us
    dot_general x66 -> x0, matrix products: 32.8 us -> none  [the longest x1 10.4 us: local(): partial_out = jnp.dot(hidden, down_w, preferred_element_type=jnp.float32)]
  transfers between devices with their start and end apart: 34 -> 0, of which waited for: 34 -> 0; matrix products, arithmetic and copies ran while one was open for 1% -> 0% of each run, Pallas kernels for 0% -> 0%
where the time goes in v1:
time: 110 us
  Pallas kernels  105 us (95%)
  local copies, waits for them, and re-layouts  5.01 us (5%)
    pallas_call x1, Pallas kernels, local(): pl.pallas_call(layer_kernel, out_shape=jax.ShapeDtypeStruct((OUTR, COLS),...  105 us
    unnamed x3, local copies, waits for them, and re-layouts  5.01 us

profile of v1, /device:TPU:1, one launch (start us, length us, event | category | flops | bytes accessed | tf_op | source)
XLA Modules:
  0.0 109.9 jit_solution(6864640048235451496)
XLA Ops:
  0.0 1.8 %copy.12.hin_hbm = bf16[512,192]{1,0:T(8,128)(2,1)} copy(bf16[512,192]{0,1:T(8,128)(2,1)} %param.11) | data formatting | bytes 393216 | tf_op args[0]
  1.8 1.9 %copy.13.wout_hbm = bf16[768,192]{1,0:T(8,128)(2,1)} copy(bf16[768,192]{0,1:T(8,128)(2,1)} %param.15) | data formatting | bytes 589824 | tf_op args[4]
  3.6 104.9 %shard_map.109 = bf16[64,192]{1,0:T(8,128)(2,1)} custom-call(s32[2,512]{1,0:T(2,128)} %bitcast.4, f32[2,512]{1,0:T(2,128)} %bitcast.5, f32[1,6144]{1,0:T(1,128)} %bitcast.3, bf16[512,768]{1,0:T(8,128)(2,1)} %q_hbm.1, bf16[512,128]{1,0:T(8,128)(2,1)} %k_hbm.1, bf16[512,128]{1,0:T(8,128)(2,1)} %v_hbm.1, bf16[512,192]{1,0:T(8,128)(2,1)} %copy.12.hin_hbm, ...), custom_call_target="tpu_custom_call" | custom-call | flops 3000000000 | bytes 12000000 | tf_op jit(solution)/shard_map/pallas_call | solution.py:488
  108.5 1.4 %copy.15 = bf16[64,192]{1,0:T(8,128)(2,1)} copy(bf16[64,192]{1,0:T(8,128)(2,1)} %shard_map.109) | data formatting | bytes 49152

commit v2 on v1

v2 whole, which is shorter than its diff:
```python
import functools
import math

import jax
import jax.numpy as jnp
from jax import lax
from jax.experimental import pallas as pl
from jax.experimental.pallas import tpu as pltpu
from jax.sharding import PartitionSpec as P

F32 = jnp.float32
BF16 = jnp.bfloat16
MESH = pl.DeviceIdType.MESH

HD = 128
D = 6144
Q = 512
CONTEXT = 16384
CHIPS = 16
ZN = 8
EN = 8
HEADS = 6
HALF = Q // 2
ROWS = HALF // CHIPS
PAIRS = ROWS * HEADS
BLK = 512
WIDE = 384
COLS = 192
SLOTS = 256
SH = SLOTS // 2
SQ = SH // 2
TOKB = HALF // EN
OUTR = Q // EN
FF = 256
MSG = PAIRS + 16
FAR = (8, 7, 9, 6, 10, 5, 11, 4, 12, 3, 13, 2, 14, 1, 15, 0)
GROUP = 4
AWAY = (4, -3, 3, -2, 2, -1, 1, 0)


def dot(a, b, dims=((1,), (0,))):
    return lax.dot_general(a, b, (dims, ((), ())), preferred_element_type=F32)


def iota(shape, dim):
    return lax.broadcasted_iota(jnp.int32, shape, dim)


def layer_kernel(
    ids_hbm, rw_hbm, gain_hbm, q_hbm, k_hbm, v_hbm, hin_hbm, wout_hbm, gate_hbm, up_hbm, down_hbm,
    out_ref,
    ids_ref, rw_ref, gain_ref, q_s, k_s, v_s, h_s, w_s, gate_s, up_s, down_s,
    sib_s, sibr_s, part_o, yin_s, num_s, got_s, own_s, att_s, ps_s, pr_s, own_p, st_s,
    xs_s, xr_s, x_s, acc_s, sq_s, part_s, ys_s, yr_s,
    h1rs, h1rr, h1ls, h1lr, h2rs, h2rr, h2ls, h2lr, h2fs, h2fr, f1s, f1r,
    o_s, os_s, or_s, rs_s, rr_s, ts_s, tr_s, town_s, tok_s,
    lsem, ssem, rsem, asem, arsem, bsem, brsem, psem, prsem, gsem, grsem, tsem, trsem,
    ysem, yrsem, xsem, xrsem, esem, ersem, ksem, krsem, vsem, vrsem,
):
    c = lax.axis_index("ctx")
    e = lax.axis_index("exp")
    core = c % 2
    chip = c // 2
    y = chip % 2
    z = chip // 2
    sib = c + 1 - 2 * core
    ypeer = c + 2 - 4 * y
    zp = [(z + d) % ZN for d in range(ZN)]

    def near(d):
        return zp[d % ZN]

    def at_chip(d, yy):
        return near(d) * 4 + yy * 2 + core

    right, left = at_chip(1, y), at_chip(-1, y)

    def owner(i):
        return near(AWAY[i % ZN]) * 2 + (1 - y if i < ZN else y)

    def remote(src, dst, send, recv, ctx=None, ex=None):
        return pltpu.make_async_remote_copy(
            src_ref=src, dst_ref=dst, send_sem=send, recv_sem=recv,
            device_id=(c if ctx is None else ctx, e if ex is None else ex),
            device_id_type=MESH,
        )

    def arrived(ref, sem):
        pltpu.make_async_copy(ref, ref, sem).wait()

    sent = []

    def push(*args, **kw):
        copy = remote(*args, **kw)
        copy.start()
        sent.append(copy)

    def drain(keep=0):
        while len(sent) > keep:
            sent.pop(0).wait_send()

    barrier = pltpu.get_barrier_semaphore()

    def greet(ctx, ex):
        pl.semaphore_signal(barrier, inc=1, device_id=(ctx, ex), device_id_type=MESH)

    greet(sib, e)
    for d in range(1, CHIPS):
        greet(2 * ((chip + d) % CHIPS) + core, e)
    for d in range(1, EN):
        greet(c, (e + d) % EN)

    half_cols = pl.ds(pl.multiple_of(HALF * core, HALF), HALF)
    sib_cols = pl.ds(pl.multiple_of(HALF * (1 - core), HALF), HALF)
    gate_h, up_h, down_h = gate_hbm.at[0], up_hbm.at[0], down_hbm.at[0]
    loads = [
        pltpu.make_async_copy(k_hbm, k_s, lsem.at[0]),
        pltpu.make_async_copy(q_hbm, q_s, lsem.at[1]),
        pltpu.make_async_copy(v_hbm, v_s, lsem.at[2]),
        pltpu.make_async_copy(hin_hbm.at[:, half_cols], h_s.at[core], lsem.at[3]),
        pltpu.make_async_copy(wout_hbm, w_s.at[core], lsem.at[4]),
        pltpu.make_async_copy(gate_h, gate_s.at[core], lsem.at[5]),
        pltpu.make_async_copy(up_h, up_s.at[core], lsem.at[6]),
        pltpu.make_async_copy(down_h, down_s.at[core], lsem.at[7]),
        pltpu.make_async_copy(ids_hbm, ids_ref, lsem.at[8]),
        pltpu.make_async_copy(rw_hbm, rw_ref, lsem.at[9]),
        pltpu.make_async_copy(gain_hbm, gain_ref, lsem.at[10]),
    ]
    for load in loads:
        load.start()

    loads[0].wait()
    loads[1].wait()
    loads[2].wait()
    keys = k_s[...]
    vals = jnp.concatenate([v_s[...], jnp.ones((BLK, HD), BF16)], axis=1)
    diag = iota((PAIRS, HD), 0) == iota((PAIRS, HD), 1)
    stat_row = iota((16, HD), 0)

    def stats_block(pk, tt):
        pk0 = pk.astype(BF16).astype(F32)
        pk1 = (pk - pk0).astype(BF16).astype(F32)
        tt0 = tt.astype(BF16).astype(F32)
        stats = jnp.where(stat_row == 0, pk0, 0.0)
        for at, term in ((1, pk1), (2, pk - pk0 - pk1), (3, tt0), (4, tt - tt0)):
            stats = jnp.where(stat_row == at, term, stats)
        return stats.astype(BF16)

    def stats_of(block):
        stats = block[PAIRS:, :].astype(F32)
        return stats[0:1] + stats[1:2] + stats[2:3], stats[3:4] + stats[4:5]

    def as_column(row):
        return jnp.sum(jnp.where(diag, row, 0.0), axis=1, keepdims=True)

    def attend(half, into, start):
        first_limit = CONTEXT - Q - BLK * c
        rows, limits = [], []
        for i in range(start, start + GROUP):
            first = HALF * half + ROWS * owner(i)
            at = pl.ds(pl.multiple_of(first, ROWS), ROWS)
            for h in range(HEADS):
                rows.append(q_s[at, HD * h : HD * (h + 1)])
                limits.append(iota((ROWS, 1), 0) + (first_limit + first))
        qg = jnp.concatenate(rows, axis=0)
        limit = jnp.concatenate(limits, axis=0)
        scores = dot(qg, keys, ((1,), (1,))) * (math.log2(math.e) / math.sqrt(HD))
        scores = jnp.where(iota(scores.shape, 1) <= limit, scores, -1e30)
        peak = jnp.max(scores, axis=1, keepdims=True)
        both = dot(jnp.exp2(scores - peak).astype(BF16), vals)
        total = both[:, HD:]
        numer = (both[:, :HD] / total).astype(BF16)
        peaks = jnp.broadcast_to(peak, total.shape)
        for g in range(GROUP):
            part = slice(PAIRS * g, PAIRS * (g + 1))
            pk = jnp.sum(jnp.where(diag, peaks[part], 0.0), axis=0, keepdims=True)
            tt = jnp.sum(jnp.where(diag, total[part], 0.0), axis=0, keepdims=True)
            into[start + g, :PAIRS, :] = numer[part]
            into[start + g, PAIRS:, :] = stats_block(pk, tt)

    for start in range(0, CHIPS, GROUP):
        attend(1 - core, sib_s, start)
    for start in range(0, CHIPS, GROUP):
        attend(core, part_o, start)

    pl.semaphore_wait(barrier, 1 + (CHIPS - 1) + (EN - 1))

    for g in range(CHIPS // GROUP):
        some = pl.ds(GROUP * g, GROUP)
        push(sib_s.at[some], sibr_s.at[some], ksem.at[g], krsem.at[g], ctx=sib)
    push(hin_hbm.at[:, sib_cols], h_s.at[core], ssem.at[2], rsem.at[2], ctx=sib)
    push(wout_hbm, w_s.at[core], ssem.at[3], rsem.at[3], ctx=sib)
    push(gate_h, gate_s.at[core], ssem.at[4], rsem.at[4], ctx=sib)
    push(up_h, up_s.at[core], ssem.at[5], rsem.at[5], ctx=sib)
    push(down_h, down_s.at[core], ssem.at[6], rsem.at[6], ctx=sib)

    def merge(blocks):
        stats = [stats_of(block) for block in blocks]
        top = functools.reduce(jnp.maximum, [pk for pk, _ in stats])
        factors = [jnp.exp2(pk - top) * tt for pk, tt in stats]
        whole = sum(factors[1:], factors[0])
        inverse = 1.0 / jnp.maximum(whole, 1e-30)
        terms = [as_column(f * inverse) * block[:PAIRS, :].astype(F32) for f, block in zip(factors, blocks)]
        return sum(terms[1:], terms[0]).astype(BF16), top, whole

    def write(into, merged):
        numer, top, whole = merged
        into[:PAIRS, :] = numer
        into[PAIRS:, :] = stats_block(top, whole)

    def sibling_arrived(i):
        if i % GROUP == 0:
            arrived(sibr_s.at[pl.ds(i, GROUP)], krsem.at[i // GROUP])

    for i in range(ZN):
        sibling_arrived(i)
        write(num_s.at[i], merge([part_o.at[i], sibr_s.at[i]]))
        push(num_s.at[i], yin_s.at[i], vsem.at[i], vrsem.at[i], ctx=ypeer)
    for i in range(ZN):
        sibling_arrived(ZN + i)
        arrived(yin_s.at[i], vrsem.at[i])
        merged = merge([part_o.at[ZN + i], sibr_s.at[ZN + i], yin_s.at[i]])
        if AWAY[i]:
            write(num_s.at[ZN + i], merged)
            push(num_s.at[ZN + i], got_s.at[z], asem.at[i], arsem.at[z], ctx=at_chip(AWAY[i], y))
        else:
            write(own_s, merged)

    loads[8].wait()
    loads[9].wait()
    ids = ids_ref[...]
    owned = jnp.where((ids[0:1] == e) | (ids[1:2] == e), 1.0, 0.0)
    w_row = jnp.where(ids[0:1] == e, rw_ref[0:1, :], 0.0) + jnp.where(ids[1:2] == e, rw_ref[1:2, :], 0.0)
    before = jnp.where(iota((Q, Q), 0) < iota((Q, Q), 1), 1.0, 0.0).astype(BF16)
    rank = dot(jnp.broadcast_to(owned, (16, Q)).astype(BF16), before)[0:1]
    place = jnp.where(owned > 0.5, rank, -1.0)
    place_col = jnp.transpose(jnp.broadcast_to(place, (HD, Q)))
    for part in range(2):
        lane = (iota((Q, SH), 1) + SH * part).astype(F32)
        tok_s[:, SH * part : SH * (part + 1)] = jnp.where(place_col == lane, 1.0, 0.0).astype(BF16)
    slot_own = (iota((SH, Q), 0) + SH * core).astype(F32)
    w_slot = jnp.sum(jnp.where(place == slot_own, w_row, 0.0), axis=1, keepdims=True)

    blocks = [own_s]
    for d in AWAY[:-1]:
        blocks.append(got_s.at[near(d)])
        arrived(blocks[-1], arsem.at[near(d)])
    att_s[chip] = merge(blocks)[0]
    for d in FAR[:-1]:
        push(att_s.at[chip], att_s.at[chip], bsem.at[d], brsem.at[chip], ctx=2 * ((chip + d) % CHIPS) + core)
    for d in range(1, CHIPS):
        source = (chip + d) % CHIPS
        arrived(att_s.at[source], brsem.at[source])

    attended = jnp.concatenate(
        [att_s[:, ROWS * h : ROWS * (h + 1), :].reshape(HALF, HD) for h in range(HEADS)], axis=1
    )
    loads[4].wait()
    arrived(w_s.at[1 - core], rsem.at[3])
    projected = dot(attended, w_s[...].reshape(WIDE, HEADS * HD), ((1,), (1,)))
    own_p[...] = projected
    ps_s[...] = projected.astype(BF16).reshape(EN, TOKB, WIDE)
    for d in range(1, EN):
        to = (e + d) % EN
        push(ps_s.at[to], pr_s.at[e], psem.at[d], prsem.at[e], ex=to)
    loads[3].wait()
    arrived(h_s.at[1 - core], rsem.at[2])
    my_tokens = jnp.where(iota((TOKB, HALF), 1) == iota((TOKB, HALF), 0) + TOKB * e, 1.0, 0.0).astype(BF16)
    before_attention = dot(my_tokens, h_s[...].reshape(WIDE, HALF), ((1,), (1,)))
    stream = own_p[pl.ds(pl.multiple_of(TOKB * e, TOKB), TOKB), :]
    for d in range(1, EN):
        source = (e + d) % EN
        arrived(pr_s.at[source], prsem.at[source])
        stream = stream + pr_s[source].astype(F32)
    stream = stream + before_attention
    st_s[e] = stream.astype(BF16)
    for d in range(1, EN):
        to = (e + d) % EN
        push(st_s.at[e], st_s.at[e], gsem.at[d], grsem.at[e], ex=to)
    for d in range(1, EN):
        source = (e + d) % EN
        arrived(st_s.at[source], grsem.at[source])

    rows = st_s[...].reshape(HALF, WIDE)

    def slots_of(part):
        token = iota((SH, HALF), 1) + HALF * core
        pick = iota((SH, HALF), 0) + SH * part
        here = jnp.where(core == 0, place[:, :HALF], place[:, HALF:])
        hot = jnp.where(here == pick.astype(F32), 1.0, 0.0).astype(BF16)
        return dot(hot, rows)

    xs_s[...] = slots_of(1 - core).astype(BF16)
    push(xs_s, xr_s, ssem.at[7], rsem.at[7], ctx=sib)
    resid = st_s[pl.ds(2 * (e % 4), 2)].reshape(OUTR, WIDE)
    take_own = jnp.where(iota((WIDE, 256), 0) == iota((WIDE, 256), 1) + COLS * core, 1.0, 0.0)
    take_sib = jnp.where(iota((WIDE, 256), 0) == iota((WIDE, 256), 1) + COLS * (1 - core), 1.0, 0.0)
    valid = iota((WIDE, 256), 1) < COLS
    take_own = jnp.where(valid, take_own, 0.0).astype(BF16)
    take_sib = jnp.where(valid, take_sib, 0.0).astype(BF16)
    rs_s[...] = dot(resid, take_sib).astype(BF16)
    push(rs_s, rr_s, ssem.at[8], rsem.at[8], ctx=sib)
    resid_own = dot(resid, take_own)
    mine = slots_of(core)
    arrived(xr_s, rsem.at[7])
    x_s[z, y] = (mine + xr_s[...].astype(F32)).astype(BF16)

    PART = SQ // 2
    low_half = pl.ds(SQ, SQ)

    def x_low(d, yy):
        return x_s.at[near(d), yy, low_half, :]

    def x_top(d, part):
        return x_s.at[near(d), :, pl.ds(PART * part, PART), :]

    def x_one(d, yy, part):
        return x_s.at[near(d), yy, pl.ds(PART * part, PART), :]

    FR, FL, TR, TL, LR, LL = (0, 2), (4, 6), (10, 13), (16, 18), 20, 23

    def first_hops(part, base, d):
        mine = x_one(0, y, part)
        for yy in (y, 1 - y):
            push(mine, mine, xsem.at[base[part] + yy], xrsem.at[base[part] + y], ctx=at_chip(d, yy))

    push(x_low(0, y), x_low(0, y), xsem.at[LL], xrsem.at[LL], ctx=left)
    first_hops(0, FR, 1)
    first_hops(1, FR, 1)
    first_hops(0, FL, -1)
    first_hops(1, FL, -1)
    push(x_low(0, y), x_low(0, y), xsem.at[LR], xrsem.at[LR], ctx=right)
    push(x_low(0, y), x_low(0, y), tsem.at[0], trsem.at[z], ctx=ypeer)
    for part in range(2):
        push(x_one(0, y, part), x_one(0, y, part), xsem.at[8 + part], xrsem.at[8 + part], ctx=ypeer)
    drain(13)

    loads[5].wait()
    loads[6].wait()
    loads[10].wait()
    arrived(gate_s.at[1 - core], rsem.at[4])
    arrived(up_s.at[1 - core], rsem.at[5])
    acc_s[...] = jnp.zeros_like(acc_s)
    sq_s[...] = jnp.zeros_like(sq_s)

    def project(d):
        zz = near(d)
        for yy in range(2):
            at = pl.ds(pl.multiple_of(WIDE * (2 * zz + yy), WIDE), WIDE)
            block = x_s[zz, yy].astype(F32)
            square = block * block
            sq_s[...] += square[:, :128] + square[:, 128:256] + square[:, 256:]
            scaled = (block * gain_ref[:, at]).astype(BF16)
            for kk in range(2):
                acc_s[0, kk] += dot(scaled, gate_s[kk, at, :])
                acc_s[1, kk] += dot(scaled, up_s[kk, at, :])

    def low_arrived(d):
        arrived(x_low(d, 1 - y), trsem.at[near(d)])

    def top_on(d, s, part, first, base, last, to):
        if s == 1:
            for yy in range(2):
                arrived(x_one(d, yy, part), xrsem.at[first[part] + yy])
        else:
            arrived(x_top(d, part), xrsem.at[base[part] + s - 2])
        if s < last:
            push(x_top(d, part), x_top(d, part), xsem.at[base[part] + s - 1], xrsem.at[base[part] + s - 1], ctx=to)

    def low_on(d, s, base, last, to):
        block = x_low(d, y)
        arrived(block, xrsem.at[base + s - 1])
        if s < last:
            push(block, block, xsem.at[base + s], xrsem.at[base + s], ctx=to)
        if s <= 3:
            push(block, block, tsem.at[d % ZN], trsem.at[near(d)], ctx=ypeer)
        if d == 3:
            push(block, block, tsem.at[4], trsem.at[near(d)], ctx=at_chip(-1, 1 - y))

    for s in range(1, 5):
        low_on(s, s, LL, 4, left)
        for part in range(2):
            top_on(-s, s, part, FR, TR, 4, right)
            if s <= 3:
                top_on(s, s, part, FL, TL, 3, left)
        if s <= 3:
            low_on(-s, s, LR, 3, right)
        if s == 1:
            for part in range(2):
                arrived(x_one(0, 1 - y, part), xrsem.at[8 + part])
            low_arrived(0)
            project(0)
        else:
            low_arrived(s - 1)
            project(s - 1)
            low_arrived(1 - s)
            project(1 - s)
    low_arrived(4)
    project(4)

    inverse_rms = lax.rsqrt(jnp.sum(sq_s[...], axis=1, keepdims=True) / D + 1e-5)
    hidden = []
    for kk in range(2):
        gate_val = acc_s[0, kk] * inverse_rms
        up_val = acc_s[1, kk] * inverse_rms
        hidden.append((gate_val / (1.0 + jnp.exp(-gate_val)) * up_val).astype(BF16))
    loads[7].wait()
    arrived(down_s.at[1 - core], rsem.at[6])

    def expand(d):
        zz = near(d)
        for yy in range(2):
            at = pl.ds(pl.multiple_of(WIDE * (2 * zz + yy), WIDE), WIDE)
            part_s[zz, yy] = dot(hidden[0], down_s[0, :, at]) + dot(hidden[1], down_s[1, :, at])
        if d == 0:
            f1s[...] = part_s[zz, 1 - y, :SQ, :].astype(BF16)
            push(f1s, f1r, ssem.at[9], rsem.at[9], ctx=ypeer)
        if d != 4:
            ys_s[zz] = part_s[zz, 1 - y, SQ:, :].astype(BF16)
            push(ys_s.at[zz], yr_s.at[zz], ysem.at[d % ZN], yrsem.at[zz], ctx=ypeer)

    def top_step(d, s, last, part, out_s, in_s, base, step):
        value = part_s[near(d), :, PART * part : PART * (part + 1), :]
        if s:
            arrived(in_s.at[s - 1, part], ersem.at[base + s - 1])
            value = value + in_s[s - 1, part].astype(F32)
        out_s[s, part] = value.astype(BF16)
        if s < last:
            push(out_s.at[s, part], in_s.at[s, part], esem.at[base + s], ersem.at[base + s], ctx=at_chip(step, y))
        else:
            for yy in (y, 1 - y):
                push(
                    out_s.at[s, part, yy], in_s.at[s, part, y],
                    esem.at[base + s + yy], ersem.at[base + s + y], ctx=at_chip(step, yy),
                )

    def top_right(s):
        for part in range(2):
            top_step(4 - s, s, 3, part, h1rs, h1rr, 5 * part, 1)

    def top_left(s):
        for part in range(2):
            top_step(s - 3, s, 2, part, h1ls, h1lr, 10 + 4 * part, -1)

    def low_value(d):
        arrived(yr_s.at[near(d)], yrsem.at[near(d)])
        return part_s[near(d), y, SQ:, :] + yr_s[near(d)].astype(F32)

    def low_right(s):
        value = low_value(3 - s)
        if s:
            arrived(h2rr.at[s - 1], ersem.at[17 + s])
            value = value + h2rr[s - 1].astype(F32)
        h2rs[s] = value.astype(BF16)
        push(h2rs.at[s], h2rr.at[s], esem.at[18 + s], ersem.at[18 + s], ctx=right)

    def low_left(s):
        if s == 0:
            h2fs[...] = part_s[near(4), :, SQ:, :].astype(BF16)
            for yy in (y, 1 - y):
                push(h2fs.at[yy], h2fr.at[y], esem.at[21 + yy], ersem.at[21 + y], ctx=at_chip(-1, yy))
            return
        value = low_value(s - 4)
        if s == 1:
            for yy in range(2):
                arrived(h2fr.at[yy], ersem.at[21 + yy])
                value = value + h2fr[yy].astype(F32)
        else:
            arrived(h2lr.at[s - 1], ersem.at[21 + s])
            value = value + h2lr[s - 1].astype(F32)
        h2ls[s] = value.astype(BF16)
        push(h2ls.at[s], h2lr.at[s], esem.at[22 + s], ersem.at[22 + s], ctx=left)

    expand(4)
    top_right(0)
    low_left(0)
    expand(-3)
    top_left(0)
    for d in (3, -2, 2, -1, 1, 0):
        expand(d)
    for s in range(1, 4):
        top_right(s)
        low_left(s)
        if s < 3:
            top_left(s)
        low_right(s - 1)
    drain(8)
    arrived(f1r, rsem.at[9])
    top_sum = part_s[z, y, :SQ, :] + f1r[...].astype(F32)
    ends = []
    for part in range(2):
        end = top_sum[PART * part : PART * (part + 1)]
        for yy in range(2):
            arrived(h1rr.at[3, part, yy], ersem.at[5 * part + 3 + yy])
            arrived(h1lr.at[2, part, yy], ersem.at[10 + 4 * part + 2 + yy])
            end = end + (h1rr[3, part, yy].astype(F32) + h1lr[2, part, yy].astype(F32))
        ends.append(end)
    low_sum = low_value(0)
    arrived(h2rr.at[2], ersem.at[20])
    arrived(h2lr.at[3], ersem.at[25])
    low_sum = low_sum + (h2rr[2].astype(F32) + h2lr[3].astype(F32))
    summed = (jnp.concatenate([*ends, low_sum], axis=0) * w_slot).astype(BF16)

    os_s[...] = dot(summed, take_sib).astype(BF16)
    push(os_s, or_s, ssem.at[10], rsem.at[10], ctx=sib)
    own_cols = dot(summed, take_own).astype(BF16)
    arrived(or_s, rsem.at[10])
    o_s[core] = own_cols
    o_s[1 - core] = or_s[...]
    slots = o_s[...].reshape(SLOTS, 256)
    town_s[...] = dot(tok_s[...], slots).reshape(EN, OUTR, 256)
    ts_s[...] = town_s[...].astype(BF16)
    for d in range(1, EN):
        to = (e + d) % EN
        push(ts_s.at[to], tr_s.at[e], psem.at[EN + d], prsem.at[EN + e], ex=to)
    arrived(rr_s, rsem.at[8])
    mixed = town_s[e] + jnp.where(core == e // 4, resid_own, rr_s[...].astype(F32))
    for d in range(1, EN):
        source = (e + d) % EN
        arrived(tr_s.at[source], prsem.at[EN + source])
        mixed = mixed + tr_s[source].astype(F32)
    out_ref[...] = mixed[:, :COLS].astype(BF16)
    drain()


def local(hidden_in, queries, keys, values, out_weight, norm_gain, expert_gate, expert_up, expert_down, expert_ids, route_weights):
    vmem = pl.BlockSpec(memory_space=pltpu.VMEM)
    anywhere = pl.BlockSpec(memory_space=pl.ANY)
    dma = pltpu.SemaphoreType.DMA

    def buf(*shape, dtype=BF16):
        return pltpu.VMEM(shape, dtype)

    scratch = [
        buf(2, Q, dtype=jnp.int32), buf(2, Q, dtype=F32), buf(1, D, dtype=F32),
        buf(Q, HEADS * HD), buf(BLK, HD), buf(BLK, HD), buf(2, COLS, HALF),
        buf(2, COLS, HEADS * HD),
        buf(2, D, FF), buf(2, D, FF), buf(2, FF, D),
        buf(CHIPS, MSG, HD), buf(CHIPS, MSG, HD), buf(CHIPS, MSG, HD),
        buf(ZN, MSG, HD), buf(CHIPS, MSG, HD), buf(ZN, MSG, HD), buf(MSG, HD), buf(CHIPS, PAIRS, HD),
        buf(EN, TOKB, WIDE), buf(EN, TOKB, WIDE), buf(HALF, WIDE, dtype=F32), buf(EN, TOKB, WIDE),
        buf(SH, WIDE), buf(SH, WIDE), buf(ZN, 2, SH, WIDE),
        buf(2, 2, SH, FF, dtype=F32), buf(SH, 128, dtype=F32), buf(ZN, 2, SH, WIDE, dtype=F32),
        buf(ZN, SQ, WIDE), buf(ZN, SQ, WIDE),
        buf(4, 2, 2, SQ // 2, WIDE), buf(4, 2, 2, SQ // 2, WIDE), buf(3, 2, 2, SQ // 2, WIDE), buf(3, 2, 2, SQ // 2, WIDE),
        buf(3, SQ, WIDE), buf(3, SQ, WIDE), buf(4, SQ, WIDE), buf(4, SQ, WIDE),
        buf(2, SQ, WIDE), buf(2, SQ, WIDE), buf(SQ, WIDE), buf(SQ, WIDE),
        buf(2, SH, 256), buf(SH, 256), buf(SH, 256), buf(OUTR, 256), buf(OUTR, 256),
        buf(EN, OUTR, 256), buf(EN, OUTR, 256), buf(EN, OUTR, 256, dtype=F32), buf(Q, SLOTS),
        dma((11,)), dma((11,)), dma((11,)),
        dma((CHIPS,)), dma((CHIPS,)), dma((CHIPS,)), dma((CHIPS,)),
        dma((2 * EN,)), dma((2 * EN,)), dma((EN,)), dma((EN,)), dma((ZN,)), dma((ZN,)),
        dma((ZN,)), dma((ZN,)), dma((27,)), dma((27,)), dma((26,)), dma((26,)), dma((4,)), dma((4,)),
        dma((ZN,)), dma((ZN,)),
    ]
    return pl.pallas_call(
        layer_kernel,
        out_shape=jax.ShapeDtypeStruct((OUTR, COLS), BF16),
        in_specs=[anywhere] * 11,
        out_specs=vmem,
        scratch_shapes=scratch,
        compiler_params=pltpu.CompilerParams(
            collective_id=0, has_side_effects=True, vmem_limit_bytes=56 * 1024 * 1024
        ),
        cost_estimate=pl.CostEstimate(flops=3 * 10**9, bytes_accessed=12 * 10**6, transcendentals=2 * 10**6),
    )(
        expert_ids.T, route_weights.T, norm_gain.reshape(1, D), queries, keys, values, hidden_in.T,
        out_weight.T, expert_gate, expert_up, expert_down,
    )


def solution(mesh):
    placed = (
        P(None, "ctx"),
        P(None, "exp"),
        P("ctx", "exp"),
        P("ctx", "exp"),
        P("exp", "ctx"),
        P(),
        P("exp", None, "ctx"),
        P("exp", None, "ctx"),
        P("exp", "ctx", None),
        P(),
        P(),
    )
    return jax.shard_map(
        local, mesh=mesh, in_specs=placed, out_specs=P("exp", "ctx"), check_vma=False
    )
```

time: 110 us -> 95 us (0.86)
  Pallas kernels: 105 us -> 93.5 us
  local copies, waits for them, and re-layouts: 5.01 us -> 1.38 us
    pallas_call x1, Pallas kernels: 105 us -> 93.5 us  [local(): pl.pallas_call(layer_kernel, out_shape=jax.ShapeDtypeStruct((OUTR, COLS),...]
    unnamed x3 -> x1, local copies, waits for them, and re-layouts: 5.01 us -> 1.38 us
where the time goes in v2:
time: 95 us; the launch traced here: 94.9 us
  Pallas kernels  93.5 us (98%)
  local copies, waits for them, and re-layouts  1.38 us (1%)
    pallas_call x1, Pallas kernels, local(): pl.pallas_call(layer_kernel, out_shape=jax.ShapeDtypeStruct((OUTR, COLS),...  93.5 us

profile of v2, /device:TPU:1, one launch (start us, length us, event | category | flops | bytes accessed | tf_op | source)
XLA Modules:
  0.0 94.9 jit_solution(3497094639985021604)
XLA Ops:
  0.0 93.5 %shard_map.109 = bf16[64,192]{1,0:T(8,128)(2,1)} custom-call(s32[2,512]{1,0:T(2,128)} %bitcast.8, f32[2,512]{1,0:T(2,128)} %bitcast.9, f32[1,6144]{1,0:T(1,128)} %bitcast.7, bf16[512,768]{1,0:T(8,128)(2,1)} %q_hbm.1, bf16[512,128]{1,0:T(8,128)(2,1)} %k_hbm.1, bf16[512,128]{1,0:T(8,128)(2,1)} %v_hbm.1, bf16[192,512]{1,0:T(8,128)(2,1)} %bitcast.6, ...), custom_call_target="tpu_custom_call" | custom-call | flops 3000000000 | bytes 12000000 | tf_op jit(solution)/shard_map/pallas_call | solution.py:556
  93.5 1.4 %copy.13 = bf16[64,192]{1,0:T(8,128)(2,1)} copy(bf16[64,192]{1,0:T(8,128)(2,1)} %shard_map.109) | data formatting | bytes 49152

commit v3 on v2

--- a/solution.py
+++ b/solution.py
@@ -32,8 +32,8 @@
 TOKB = HALF // EN
 OUTR = Q // EN
 FF = 256
+PACK = OUTR + OUTR // 2
 MSG = PAIRS + 16
-FAR = (8, 7, 9, 6, 10, 5, 11, 4, 12, 3, 13, 2, 14, 1, 15, 0)
 GROUP = 4
 AWAY = (4, -3, 3, -2, 2, -1, 1, 0)
 
@@ -54,8 +54,7 @@
     xs_s, xr_s, x_s, acc_s, sq_s, part_s, ys_s, yr_s,
     h1rs, h1rr, h1ls, h1lr, h2rs, h2rr, h2ls, h2lr, h2fs, h2fr, f1s, f1r,
     o_s, os_s, or_s, rs_s, rr_s, ts_s, tr_s, town_s, tok_s,
-    lsem, ssem, rsem, asem, arsem, bsem, brsem, psem, prsem, gsem, grsem, tsem, trsem,
-    ysem, yrsem, xsem, xrsem, esem, ersem, ksem, krsem, vsem, vrsem,
+    lsem, ssem, rsem, tosem, krsem, vrsem, arsem, brsem, prsem, trsem, yrsem, xrsem, ersem,
 ):
     c = lax.axis_index("ctx")
     e = lax.axis_index("exp")
@@ -95,9 +94,14 @@
         copy.start()
         sent.append(copy)
 
-    def drain(keep=0):
-        while len(sent) > keep:
-            sent.pop(0).wait_send()
+    (TO_SIB, TO_Y, TO_Z, TO_CHIPS, TO_EXP, TO_EXP_ALL, TO_LOW_Y, TO_FIRST, TO_PAIRS, TO_LOW, TO_SUM_Y,
+     TO_TR, TO_TL, TO_LR, TO_LF, TO_LL, TO_TOK) = range(17)
+
+    def send(src, dst, kind, recv, **kw):
+        remote(src, dst, tosem.at[kind], recv, **kw).start()
+
+    def left_here(ref, kind):
+        remote(ref, ref, tosem.at[kind], tosem.at[kind], ctx=sib).wait_send()
 
     barrier = pltpu.get_barrier_semaphore()
 
@@ -187,7 +191,7 @@
 
     for g in range(CHIPS // GROUP):
         some = pl.ds(GROUP * g, GROUP)
-        push(sib_s.at[some], sibr_s.at[some], ksem.at[g], krsem.at[g], ctx=sib)
+        send(sib_s.at[some], sibr_s.at[some], TO_SIB, krsem.at[g], ctx=sib)
     push(hin_hbm.at[:, sib_cols], h_s.at[core], ssem.at[2], rsem.at[2], ctx=sib)
     push(wout_hbm, w_s.at[core], ssem.at[3], rsem.at[3], ctx=sib)
     push(gate_h, gate_s.at[core], ssem.at[4], rsem.at[4], ctx=sib)
@@ -215,14 +219,14 @@
     for i in range(ZN):
         sibling_arrived(i)
         write(num_s.at[i], merge([part_o.at[i], sibr_s.at[i]]))
-        push(num_s.at[i], yin_s.at[i], vsem.at[i], vrsem.at[i], ctx=ypeer)
+        send(num_s.at[i], yin_s.at[i], TO_Y, vrsem.at[i], ctx=ypeer)
     for i in range(ZN):
         sibling_arrived(ZN + i)
         arrived(yin_s.at[i], vrsem.at[i])
         merged = merge([part_o.at[ZN + i], sibr_s.at[ZN + i], yin_s.at[i]])
         if AWAY[i]:
             write(num_s.at[ZN + i], merged)
-            push(num_s.at[ZN + i], got_s.at[z], asem.at[i], arsem.at[z], ctx=at_chip(AWAY[i], y))
+            send(num_s.at[ZN + i], got_s.at[z], TO_Z, arsem.at[0], ctx=at_chip(AWAY[i], y))
         else:
             write(own_s, merged)
 
@@ -241,45 +245,50 @@
     slot_own = (iota((SH, Q), 0) + SH * core).astype(F32)
     w_slot = jnp.sum(jnp.where(place == slot_own, w_row, 0.0), axis=1, keepdims=True)
 
-    blocks = [own_s]
-    for d in AWAY[:-1]:
-        blocks.append(got_s.at[near(d)])
-        arrived(blocks[-1], arsem.at[near(d)])
-    att_s[chip] = merge(blocks)[0]
-    for d in FAR[:-1]:
-        push(att_s.at[chip], att_s.at[chip], bsem.at[d], brsem.at[chip], ctx=2 * ((chip + d) % CHIPS) + core)
-    for d in range(1, CHIPS):
-        source = (chip + d) % CHIPS
-        arrived(att_s.at[source], brsem.at[source])
-
-    attended = jnp.concatenate(
-        [att_s[:, ROWS * h : ROWS * (h + 1), :].reshape(HALF, HD) for h in range(HEADS)], axis=1
-    )
+    arrived(got_s.at[pl.ds(0, ZN - 1)], arsem.at[0])
+    att_s[chip] = merge([own_s] + [got_s.at[near(d)] for d in AWAY[:-1]])[0]
+    for d in AWAY:
+        for yy in (y, 1 - y):
+            if d or yy is not y:
+                send(att_s.at[chip], att_s.at[chip], TO_CHIPS, brsem.at[chip], ctx=at_chip(d, yy))
+
     loads[4].wait()
     arrived(w_s.at[1 - core], rsem.at[3])
-    projected = dot(attended, w_s[...].reshape(WIDE, HEADS * HD), ((1,), (1,)))
-    own_p[...] = projected
-    ps_s[...] = projected.astype(BF16).reshape(EN, TOKB, WIDE)
-    for d in range(1, EN):
-        to = (e + d) % EN
-        push(ps_s.at[to], pr_s.at[e], psem.at[d], prsem.at[e], ex=to)
+    weight = w_s[...].reshape(WIDE, HEADS * HD)
+    for d in (0, *AWAY[:-1]):
+        to = near(d)
+        for source in (2 * to, 2 * to + 1) if d else (2 * z + 1 - y,):
+            arrived(att_s.at[source], brsem.at[source])
+        pair = att_s[pl.ds(2 * to, 2)]
+        attended = jnp.concatenate(
+            [pair[:, ROWS * h : ROWS * (h + 1), :].reshape(TOKB, HD) for h in range(HEADS)], axis=1
+        )
+        projected = dot(attended, weight, ((1,), (1,)))
+        ps_s[to] = projected.astype(BF16)
+
+        @pl.when(to == e)
+        def _(projected=projected):
+            own_p[...] = projected
+
+        @pl.when(to != e)
+        def _(to=to):
+            send(ps_s.at[to], pr_s.at[e], TO_EXP, prsem.at[0], ex=to)
+
     loads[3].wait()
     arrived(h_s.at[1 - core], rsem.at[2])
     my_tokens = jnp.where(iota((TOKB, HALF), 1) == iota((TOKB, HALF), 0) + TOKB * e, 1.0, 0.0).astype(BF16)
     before_attention = dot(my_tokens, h_s[...].reshape(WIDE, HALF), ((1,), (1,)))
-    stream = own_p[pl.ds(pl.multiple_of(TOKB * e, TOKB), TOKB), :]
+    stream = own_p[...]
+    arrived(pr_s.at[pl.ds(0, EN - 1)], prsem.at[0])
     for d in range(1, EN):
         source = (e + d) % EN
-        arrived(pr_s.at[source], prsem.at[source])
         stream = stream + pr_s[source].astype(F32)
     stream = stream + before_attention
     st_s[e] = stream.astype(BF16)
     for d in range(1, EN):
         to = (e + d) % EN
-        push(st_s.at[e], st_s.at[e], gsem.at[d], grsem.at[e], ex=to)
-    for d in range(1, EN):
-        source = (e + d) % EN
-        arrived(st_s.at[source], grsem.at[source])
+        send(st_s.at[e], st_s.at[e], TO_EXP_ALL, prsem.at[1], ex=to)
+    arrived(st_s.at[pl.ds(0, EN - 1)], prsem.at[1])
 
     rows = st_s[...].reshape(HALF, WIDE)
 
@@ -317,23 +326,24 @@
     def x_one(d, yy, part):
         return x_s.at[near(d), yy, pl.ds(PART * part, PART), :]
 
-    FR, FL, TR, TL, LR, LL = (0, 2), (4, 6), (10, 13), (16, 18), 20, 23
+    FR, FL, OY, TR, TL, LR, LL = 0, 2, 4, (6, 9), (12, 14), 16, 19
+
+    def same(block, kind, recv, to):
+        send(block, block, kind, recv, ctx=to)
 
     def first_hops(part, base, d):
-        mine = x_one(0, y, part)
         for yy in (y, 1 - y):
-            push(mine, mine, xsem.at[base[part] + yy], xrsem.at[base[part] + y], ctx=at_chip(d, yy))
-
-    push(x_low(0, y), x_low(0, y), xsem.at[LL], xrsem.at[LL], ctx=left)
+            same(x_one(0, y, part), TO_FIRST, xrsem.at[base + part], at_chip(d, yy))
+
+    same(x_low(0, y), TO_LOW, xrsem.at[LL], left)
     first_hops(0, FR, 1)
     first_hops(1, FR, 1)
     first_hops(0, FL, -1)
     first_hops(1, FL, -1)
-    push(x_low(0, y), x_low(0, y), xsem.at[LR], xrsem.at[LR], ctx=right)
-    push(x_low(0, y), x_low(0, y), tsem.at[0], trsem.at[z], ctx=ypeer)
+    same(x_low(0, y), TO_LOW, xrsem.at[LR], right)
+    same(x_low(0, y), TO_LOW_Y, trsem.at[z], ypeer)
     for part in range(2):
-        push(x_one(0, y, part), x_one(0, y, part), xsem.at[8 + part], xrsem.at[8 + part], ctx=ypeer)
-    drain(13)
+        same(x_one(0, y, part), TO_FIRST, xrsem.at[OY + part], ypeer)
 
     loads[5].wait()
     loads[6].wait()
@@ -359,23 +369,19 @@
         arrived(x_low(d, 1 - y), trsem.at[near(d)])
 
     def top_on(d, s, part, first, base, last, to):
-        if s == 1:
-            for yy in range(2):
-                arrived(x_one(d, yy, part), xrsem.at[first[part] + yy])
-        else:
-            arrived(x_top(d, part), xrsem.at[base[part] + s - 2])
+        arrived(x_top(d, part), xrsem.at[first + part if s == 1 else base[part] + s - 2])
         if s < last:
-            push(x_top(d, part), x_top(d, part), xsem.at[base[part] + s - 1], xrsem.at[base[part] + s - 1], ctx=to)
+            same(x_top(d, part), TO_PAIRS, xrsem.at[base[part] + s - 1], to)
 
     def low_on(d, s, base, last, to):
         block = x_low(d, y)
         arrived(block, xrsem.at[base + s - 1])
         if s < last:
-            push(block, block, xsem.at[base + s], xrsem.at[base + s], ctx=to)
+            same(block, TO_LOW, xrsem.at[base + s], to)
         if s <= 3:
-            push(block, block, tsem.at[d % ZN], trsem.at[near(d)], ctx=ypeer)
+            same(block, TO_LOW_Y, trsem.at[near(d)], ypeer)
         if d == 3:
-            push(block, block, tsem.at[4], trsem.at[near(d)], ctx=at_chip(-1, 1 - y))
+            same(block, TO_LOW_Y, trsem.at[near(d)], at_chip(-1, 1 - y))
 
     for s in range(1, 5):
         low_on(s, s, LL, 4, left)
@@ -387,7 +393,7 @@
             low_on(-s, s, LR, 3, right)
         if s == 1:
             for part in range(2):
-                arrived(x_one(0, 1 - y, part), xrsem.at[8 + part])
+                arrived(x_one(0, 1 - y, part), xrsem.at[OY + part])
             low_arrived(0)
             project(0)
         else:
@@ -417,30 +423,27 @@
             push(f1s, f1r, ssem.at[9], rsem.at[9], ctx=ypeer)
         if d != 4:
             ys_s[zz] = part_s[zz, 1 - y, SQ:, :].astype(BF16)
-            push(ys_s.at[zz], yr_s.at[zz], ysem.at[d % ZN], yrsem.at[zz], ctx=ypeer)
-
-    def top_step(d, s, last, part, out_s, in_s, base, step):
+            send(ys_s.at[zz], yr_s.at[zz], TO_SUM_Y, yrsem.at[zz], ctx=ypeer)
+
+    def top_step(d, s, last, part, out_s, in_s, kind, base, step):
         value = part_s[near(d), :, PART * part : PART * (part + 1), :]
         if s:
             arrived(in_s.at[s - 1, part], ersem.at[base + s - 1])
             value = value + in_s[s - 1, part].astype(F32)
         out_s[s, part] = value.astype(BF16)
         if s < last:
-            push(out_s.at[s, part], in_s.at[s, part], esem.at[base + s], ersem.at[base + s], ctx=at_chip(step, y))
+            send(out_s.at[s, part], in_s.at[s, part], kind, ersem.at[base + s], ctx=at_chip(step, y))
         else:
             for yy in (y, 1 - y):
-                push(
-                    out_s.at[s, part, yy], in_s.at[s, part, y],
-                    esem.at[base + s + yy], ersem.at[base + s + y], ctx=at_chip(step, yy),
-                )
+                send(out_s.at[s, part, yy], in_s.at[s, part, y], kind, ersem.at[base + s], ctx=at_chip(step, yy))
 
     def top_right(s):
         for part in range(2):
-            top_step(4 - s, s, 3, part, h1rs, h1rr, 5 * part, 1)
+            top_step(4 - s, s, 3, part, h1rs, h1rr, TO_TR, 4 * part, 1)
 
     def top_left(s):
         for part in range(2):
-            top_step(s - 3, s, 2, part, h1ls, h1lr, 10 + 4 * part, -1)
+            top_step(s - 3, s, 2, part, h1ls, h1lr, TO_TL, 8 + 3 * part, -1)
 
     def low_value(d):
         arrived(yr_s.at[near(d)], yrsem.at[near(d)])
@@ -449,27 +452,26 @@
     def low_right(s):
         value = low_value(3 - s)
         if s:
-            arrived(h2rr.at[s - 1], ersem.at[17 + s])
+            arrived(h2rr.at[s - 1], ersem.at[13 + s])
             value = value + h2rr[s - 1].astype(F32)
         h2rs[s] = value.astype(BF16)
-        push(h2rs.at[s], h2rr.at[s], esem.at[18 + s], ersem.at[18 + s], ctx=right)
+        send(h2rs.at[s], h2rr.at[s], TO_LR, ersem.at[14 + s], ctx=right)
 
     def low_left(s):
         if s == 0:
             h2fs[...] = part_s[near(4), :, SQ:, :].astype(BF16)
             for yy in (y, 1 - y):
-                push(h2fs.at[yy], h2fr.at[y], esem.at[21 + yy], ersem.at[21 + y], ctx=at_chip(-1, yy))
+                send(h2fs.at[yy], h2fr.at[y], TO_LF, ersem.at[17], ctx=at_chip(-1, yy))
             return
         value = low_value(s - 4)
         if s == 1:
-            for yy in range(2):
-                arrived(h2fr.at[yy], ersem.at[21 + yy])
-                value = value + h2fr[yy].astype(F32)
+            arrived(h2fr, ersem.at[17])
+            value = value + (h2fr[0].astype(F32) + h2fr[1].astype(F32))
         else:
-            arrived(h2lr.at[s - 1], ersem.at[21 + s])
-            value = value + h2lr[s - 1].astype(F32)
-        h2ls[s] = value.astype(BF16)
-        push(h2ls.at[s], h2lr.at[s], esem.at[22 + s], ersem.at[22 + s], ctx=left)
+            arrived(h2lr.at[s - 2], ersem.at[16 + s])
+            value = value + h2lr[s - 2].astype(F32)
+        h2ls[s - 1] = value.astype(BF16)
+        send(h2ls.at[s - 1], h2lr.at[s - 1], TO_LL, ersem.at[17 + s], ctx=left)
 
     expand(4)
     top_right(0)
@@ -484,21 +486,20 @@
         if s < 3:
             top_left(s)
         low_right(s - 1)
-    drain(8)
     arrived(f1r, rsem.at[9])
     top_sum = part_s[z, y, :SQ, :] + f1r[...].astype(F32)
     ends = []
     for part in range(2):
         end = top_sum[PART * part : PART * (part + 1)]
+        arrived(h1rr.at[3, part], ersem.at[4 * part + 3])
+        arrived(h1lr.at[2, part], ersem.at[8 + 3 * part + 2])
         for yy in range(2):
-            arrived(h1rr.at[3, part, yy], ersem.at[5 * part + 3 + yy])
-            arrived(h1lr.at[2, part, yy], ersem.at[10 + 4 * part + 2 + yy])
             end = end + (h1rr[3, part, yy].astype(F32) + h1lr[2, part, yy].astype(F32))
         ends.append(end)
     low_sum = low_value(0)
-    arrived(h2rr.at[2], ersem.at[20])
-    arrived(h2lr.at[3], ersem.at[25])
-    low_sum = low_sum + (h2rr[2].astype(F32) + h2lr[3].astype(F32))
+    arrived(h2rr.at[2], ersem.at[16])
+    arrived(h2lr.at[2], ersem.at[20])
+    low_sum = low_sum + (h2rr[2].astype(F32) + h2lr[2].astype(F32))
     summed = (jnp.concatenate([*ends, low_sum], axis=0) * w_slot).astype(BF16)
 
     os_s[...] = dot(summed, take_sib).astype(BF16)
@@ -508,24 +509,41 @@
     o_s[core] = own_cols
     o_s[1 - core] = or_s[...]
     slots = o_s[...].reshape(SLOTS, 256)
-    town_s[...] = dot(tok_s[...], slots).reshape(EN, OUTR, 256)
-    ts_s[...] = town_s[...].astype(BF16)
+    terms = dot(tok_s[...], slots).reshape(EN, OUTR, 256)
+    tails = pltpu.roll(terms[:, TOKB:, HD:].reshape(HALF, HD), 64, 1).reshape(EN, TOKB, HD)
+    terms = jnp.concatenate([terms[:, :, :HD], terms[:, :TOKB, HD:] + tails], axis=1)
+    town_s[...] = terms
+    ts_s[...] = terms.astype(BF16)
     for d in range(1, EN):
         to = (e + d) % EN
-        push(ts_s.at[to], tr_s.at[e], psem.at[EN + d], prsem.at[EN + e], ex=to)
+        send(ts_s.at[to], tr_s.at[e], TO_TOK, prsem.at[2], ex=to)
     arrived(rr_s, rsem.at[8])
-    mixed = town_s[e] + jnp.where(core == e // 4, resid_own, rr_s[...].astype(F32))
+    resid = jnp.where(core == e // 4, resid_own, rr_s[...].astype(F32))
+    mixed = town_s[e]
+    arrived(tr_s.at[pl.ds(0, EN - 1)], prsem.at[2])
     for d in range(1, EN):
-        source = (e + d) % EN
-        arrived(tr_s.at[source], prsem.at[EN + source])
-        mixed = mixed + tr_s[source].astype(F32)
+        mixed = mixed + tr_s[(e + d) % EN].astype(F32)
+    tail = mixed[OUTR:]
+    tail = jnp.concatenate([tail, pltpu.roll(tail, 64, 1)], axis=0)
+    mixed = jnp.concatenate([mixed[:OUTR], tail], axis=1) + resid
     out_ref[...] = mixed[:, :COLS].astype(BF16)
-    drain()
+    for copy in sent:
+        copy.wait_send()
+    for ref, kind in (
+        (sib_s, TO_SIB), (num_s.at[pl.ds(0, ZN)], TO_Y), (num_s.at[pl.ds(ZN, ZN - 1)], TO_Z),
+        (att_s.at[pl.ds(0, CHIPS - 1)], TO_CHIPS), (ps_s.at[pl.ds(0, EN - 1)], TO_EXP),
+        (st_s.at[pl.ds(0, EN - 1)], TO_EXP_ALL), (x_s.at[:, 0, low_half, :], TO_LOW_Y),
+        (x_s.at[pl.ds(0, 5), 0, low_half, :], TO_FIRST), (x_s.at[pl.ds(0, 5), 0], TO_PAIRS),
+        (x_s.at[pl.ds(0, 7), 0, low_half, :], TO_LOW), (ys_s.at[pl.ds(0, ZN - 1)], TO_SUM_Y),
+        (h1rs, TO_TR), (h1ls, TO_TL), (h2rs, TO_LR), (h2fs, TO_LF), (h2ls, TO_LL),
+        (ts_s.at[pl.ds(0, EN - 1)], TO_TOK),
+    ):
+        left_here(ref, kind)
 
 
 def local(hidden_in, queries, keys, values, out_weight, norm_gain, expert_gate, expert_up, expert_down, expert_ids, route_weights):
     vmem = pl.BlockSpec(memory_space=pltpu.VMEM)
-    anywhere = pl.BlockSpec(memory_space=pl.ANY)
+    anywhere = pl.BlockSpec(memory_space=pltpu.HBM)
     dma = pltpu.SemaphoreType.DMA
 
     def buf(*shape, dtype=BF16):
@@ -538,20 +556,17 @@
         buf(2, D, FF), buf(2, D, FF), buf(2, FF, D),
         buf(CHIPS, MSG, HD), buf(CHIPS, MSG, HD), buf(CHIPS, MSG, HD),
         buf(ZN, MSG, HD), buf(CHIPS, MSG, HD), buf(ZN, MSG, HD), buf(MSG, HD), buf(CHIPS, PAIRS, HD),
-        buf(EN, TOKB, WIDE), buf(EN, TOKB, WIDE), buf(HALF, WIDE, dtype=F32), buf(EN, TOKB, WIDE),
+        buf(EN, TOKB, WIDE), buf(EN, TOKB, WIDE), buf(TOKB, WIDE, dtype=F32), buf(EN, TOKB, WIDE),
         buf(SH, WIDE), buf(SH, WIDE), buf(ZN, 2, SH, WIDE),
         buf(2, 2, SH, FF, dtype=F32), buf(SH, 128, dtype=F32), buf(ZN, 2, SH, WIDE, dtype=F32),
         buf(ZN, SQ, WIDE), buf(ZN, SQ, WIDE),
         buf(4, 2, 2, SQ // 2, WIDE), buf(4, 2, 2, SQ // 2, WIDE), buf(3, 2, 2, SQ // 2, WIDE), buf(3, 2, 2, SQ // 2, WIDE),
-        buf(3, SQ, WIDE), buf(3, SQ, WIDE), buf(4, SQ, WIDE), buf(4, SQ, WIDE),
+        buf(3, SQ, WIDE), buf(3, SQ, WIDE), buf(3, SQ, WIDE), buf(3, SQ, WIDE),
         buf(2, SQ, WIDE), buf(2, SQ, WIDE), buf(SQ, WIDE), buf(SQ, WIDE),
         buf(2, SH, 256), buf(SH, 256), buf(SH, 256), buf(OUTR, 256), buf(OUTR, 256),
-        buf(EN, OUTR, 256), buf(EN, OUTR, 256), buf(EN, OUTR, 256, dtype=F32), buf(Q, SLOTS),
-        dma((11,)), dma((11,)), dma((11,)),
-        dma((CHIPS,)), dma((CHIPS,)), dma((CHIPS,)), dma((CHIPS,)),
-        dma((2 * EN,)), dma((2 * EN,)), dma((EN,)), dma((EN,)), dma((ZN,)), dma((ZN,)),
-        dma((ZN,)), dma((ZN,)), dma((27,)), dma((27,)), dma((26,)), dma((26,)), dma((4,)), dma((4,)),
-        dma((ZN,)), dma((ZN,)),
+        buf(EN, PACK, HD), buf(EN, PACK, HD), buf(EN, PACK, HD, dtype=F32), buf(Q, SLOTS),
+        dma((11,)), dma((11,)), dma((11,)), dma((17,)), dma((4,)), dma((ZN,)), dma((1,)), dma((CHIPS,)),
+        dma((3,)), dma((ZN,)), dma((ZN,)), dma((23,)), dma((21,)),
     ]
     return pl.pallas_call(
         layer_kernel,
@@ -560,12 +575,17 @@
         out_specs=vmem,
         scratch_shapes=scratch,
         compiler_params=pltpu.CompilerParams(
-            collective_id=0, has_side_effects=True, vmem_limit_bytes=56 * 1024 * 1024
+            collective_id=0, has_side_effects=True, vmem_limit_bytes=40 * 1024 * 1024
         ),
         cost_estimate=pl.CostEstimate(flops=3 * 10**9, bytes_accessed=12 * 10**6, transcendentals=2 * 10**6),
     )(
-        expert_ids.T, route_weights.T, norm_gain.reshape(1, D), queries, keys, values, hidden_in.T,
-        out_weight.T, expert_gate, expert_up, expert_down,
+        *(
+            pltpu.with_memory_space_constraint(x, pltpu.HBM)
+            for x in (
+                expert_ids.T, route_weights.T, norm_gain.reshape(1, D), queries, keys, values, hidden_in.T,
+                out_weight.T, expert_gate, expert_up, expert_down,
+            )
+        )
     )
 
 

time: 95 us -> 91.8 us (0.966)
  Pallas kernels: 93.5 us -> 91.1 us
    pallas_call x1, Pallas kernels: 93.5 us -> 91.1 us  [local(): pl.pallas_call(layer_kernel, out_shape=jax.ShapeDtypeStruct((OUTR, COLS),...]
where the time goes in v3:
time: 91.8 us
  Pallas kernels  91.1 us (99%)
    pallas_call x1, Pallas kernels, local(): pl.pallas_call(layer_kernel, out_shape=jax.ShapeDtypeStruct((OUTR, COLS),...  91.1 us

profile of v3, /device:TPU:1, one launch (start us, length us, event | category | flops | bytes accessed | tf_op | source)
XLA Modules:
  0.0 91.8 jit_solution(14817940620493520716)
XLA Ops:
  0.0 91.1 %shard_map.109 = bf16[64,192]{1,0:T(8,128)(2,1)S(1)} custom-call(s32[2,512]{1,0:T(2,128)} %bitcast.8, f32[2,512]{1,0:T(2,128)} %bitcast.9, f32[1,6144]{1,0:T(1,128)} %bitcast.7, bf16[512,768]{1,0:T(8,128)(2,1)} %q_hbm.1, bf16[512,128]{1,0:T(8,128)(2,1)} %k_hbm.1, bf16[512,128]{1,0:T(8,128)(2,1)} %v_hbm.1, bf16[192,512]{1,0:T(8,128)(2,1)} %bitcast.6, ...), custom_call_target="tpu_custom_call" | custom-call | flops 3000000000 | bytes 12000000 | tf_op jit(solution)/shard_map/pallas_call | solution.py:571
  91.1 0.6 copy.13

commit v4 on v3

--- a/solution.py
+++ b/solution.py
@@ -35,7 +35,10 @@
 PACK = OUTR + OUTR // 2
 MSG = PAIRS + 16
 GROUP = 4
+PARTS = 2
+PART = SQ // PARTS
 AWAY = (4, -3, 3, -2, 2, -1, 1, 0)
+FAR = AWAY[:3]
 
 
 def dot(a, b, dims=((1,), (0,))):
@@ -53,7 +56,7 @@
     sib_s, sibr_s, part_o, yin_s, num_s, got_s, own_s, att_s, ps_s, pr_s, own_p, st_s,
     xs_s, xr_s, x_s, acc_s, sq_s, part_s, ys_s, yr_s,
     h1rs, h1rr, h1ls, h1lr, h2rs, h2rr, h2ls, h2lr, h2fs, h2fr, f1s, f1r,
-    o_s, os_s, or_s, rs_s, rr_s, ts_s, tr_s, town_s, tok_s,
+    o_s, os_s, or_s, hot_s, take_s, ro_s, rs_s, rr_s, ts_s, tr_s, town_s, tok_s,
     lsem, ssem, rsem, tosem, krsem, vrsem, arsem, brsem, prsem, trsem, yrsem, xrsem, ersem,
 ):
     c = lax.axis_index("ctx")
@@ -245,19 +248,29 @@
     slot_own = (iota((SH, Q), 0) + SH * core).astype(F32)
     w_slot = jnp.sum(jnp.where(place == slot_own, w_row, 0.0), axis=1, keepdims=True)
 
+    here = jnp.where(core == 0, place[:, :HALF], place[:, HALF:])
+    for part in range(2):
+        pick = (iota((SH, HALF), 0) + SH * part).astype(F32)
+        hot_s[part] = jnp.where(here == pick, 1.0, 0.0).astype(BF16)
+
     arrived(got_s.at[pl.ds(0, ZN - 1)], arsem.at[0])
     att_s[chip] = merge([own_s] + [got_s.at[near(d)] for d in AWAY[:-1]])[0]
     for d in AWAY:
         for yy in (y, 1 - y):
-            if d or yy is not y:
-                send(att_s.at[chip], att_s.at[chip], TO_CHIPS, brsem.at[chip], ctx=at_chip(d, yy))
+            if yy is y and d == 0 or yy is not y and d in FAR:
+                continue
+            send(att_s.at[chip], att_s.at[chip], TO_CHIPS, brsem.at[chip], ctx=at_chip(d, yy))
+    for d in FAR:
+        source = 2 * near(d) + y
+        arrived(att_s.at[source], brsem.at[source])
+        send(att_s.at[source], att_s.at[source], TO_CHIPS, brsem.at[source], ctx=ypeer)
 
     loads[4].wait()
     arrived(w_s.at[1 - core], rsem.at[3])
     weight = w_s[...].reshape(WIDE, HEADS * HD)
-    for d in (0, *AWAY[:-1]):
+    for d in (0, *AWAY[3:-1], *FAR):
         to = near(d)
-        for source in (2 * to, 2 * to + 1) if d else (2 * z + 1 - y,):
+        for source in (2 * to, 2 * to + 1) if d and d not in FAR else (2 * to + 1 - y,):
             arrived(att_s.at[source], brsem.at[source])
         pair = att_s[pl.ds(2 * to, 2)]
         attended = jnp.concatenate(
@@ -292,58 +305,53 @@
 
     rows = st_s[...].reshape(HALF, WIDE)
 
-    def slots_of(part):
-        token = iota((SH, HALF), 1) + HALF * core
-        pick = iota((SH, HALF), 0) + SH * part
-        here = jnp.where(core == 0, place[:, :HALF], place[:, HALF:])
-        hot = jnp.where(here == pick.astype(F32), 1.0, 0.0).astype(BF16)
-        return dot(hot, rows)
-
-    xs_s[...] = slots_of(1 - core).astype(BF16)
+    xs_s[...] = dot(hot_s[1 - core], rows).astype(BF16)
     push(xs_s, xr_s, ssem.at[7], rsem.at[7], ctx=sib)
+    mine = dot(hot_s[core], rows)
+    arrived(xr_s, rsem.at[7])
+    x_s[z, y] = (mine + xr_s[...].astype(F32)).astype(BF16)
+
+    low_half = pl.ds(SQ, SQ)
+
+    def x_low(d, yy):
+        return x_s.at[near(d), yy, low_half, :]
+
+    def x_top(d, part):
+        return x_s.at[near(d), :, pl.ds(PART * part, PART), :]
+
+    def x_one(d, yy, part):
+        return x_s.at[near(d), yy, pl.ds(PART * part, PART), :]
+
+    FR, FL, OY = 0, PARTS, 2 * PARTS
+    TR = [3 * PARTS + 3 * part for part in range(PARTS)]
+    TL = [6 * PARTS + 2 * part for part in range(PARTS)]
+    LR, LL = 8 * PARTS, 8 * PARTS + 3
+
+    def same(block, kind, recv, to):
+        send(block, block, kind, recv, ctx=to)
+
+    def first_hops(part, base, d):
+        for yy in (y, 1 - y):
+            same(x_one(0, y, part), TO_FIRST, xrsem.at[base + part], at_chip(d, yy))
+
+    same(x_low(0, y), TO_LOW, xrsem.at[LL], left)
+    for part in range(PARTS):
+        first_hops(part, FR, 1)
+        first_hops(part, FL, -1)
+    same(x_low(0, y), TO_LOW, xrsem.at[LR], right)
+    same(x_low(0, y), TO_LOW_Y, trsem.at[z], ypeer)
+    for part in range(PARTS):
+        same(x_one(0, y, part), TO_FIRST, xrsem.at[OY + part], ypeer)
+
     resid = st_s[pl.ds(2 * (e % 4), 2)].reshape(OUTR, WIDE)
     take_own = jnp.where(iota((WIDE, 256), 0) == iota((WIDE, 256), 1) + COLS * core, 1.0, 0.0)
     take_sib = jnp.where(iota((WIDE, 256), 0) == iota((WIDE, 256), 1) + COLS * (1 - core), 1.0, 0.0)
     valid = iota((WIDE, 256), 1) < COLS
-    take_own = jnp.where(valid, take_own, 0.0).astype(BF16)
-    take_sib = jnp.where(valid, take_sib, 0.0).astype(BF16)
-    rs_s[...] = dot(resid, take_sib).astype(BF16)
+    take_s[0] = jnp.where(valid, take_own, 0.0).astype(BF16)
+    take_s[1] = jnp.where(valid, take_sib, 0.0).astype(BF16)
+    rs_s[...] = dot(resid, take_s[1]).astype(BF16)
     push(rs_s, rr_s, ssem.at[8], rsem.at[8], ctx=sib)
-    resid_own = dot(resid, take_own)
-    mine = slots_of(core)
-    arrived(xr_s, rsem.at[7])
-    x_s[z, y] = (mine + xr_s[...].astype(F32)).astype(BF16)
-
-    PART = SQ // 2
-    low_half = pl.ds(SQ, SQ)
-
-    def x_low(d, yy):
-        return x_s.at[near(d), yy, low_half, :]
-
-    def x_top(d, part):
-        return x_s.at[near(d), :, pl.ds(PART * part, PART), :]
-
-    def x_one(d, yy, part):
-        return x_s.at[near(d), yy, pl.ds(PART * part, PART), :]
-
-    FR, FL, OY, TR, TL, LR, LL = 0, 2, 4, (6, 9), (12, 14), 16, 19
-
-    def same(block, kind, recv, to):
-        send(block, block, kind, recv, ctx=to)
-
-    def first_hops(part, base, d):
-        for yy in (y, 1 - y):
-            same(x_one(0, y, part), TO_FIRST, xrsem.at[base + part], at_chip(d, yy))
-
-    same(x_low(0, y), TO_LOW, xrsem.at[LL], left)
-    first_hops(0, FR, 1)
-    first_hops(1, FR, 1)
-    first_hops(0, FL, -1)
-    first_hops(1, FL, -1)
-    same(x_low(0, y), TO_LOW, xrsem.at[LR], right)
-    same(x_low(0, y), TO_LOW_Y, trsem.at[z], ypeer)
-    for part in range(2):
-        same(x_one(0, y, part), TO_FIRST, xrsem.at[OY + part], ypeer)
+    ro_s[...] = dot(resid, take_s[0])
 
     loads[5].wait()
     loads[6].wait()
@@ -385,14 +393,14 @@
 
     for s in range(1, 5):
         low_on(s, s, LL, 4, left)
-        for part in range(2):
+        for part in range(PARTS):
             top_on(-s, s, part, FR, TR, 4, right)
             if s <= 3:
                 top_on(s, s, part, FL, TL, 3, left)
         if s <= 3:
             low_on(-s, s, LR, 3, right)
         if s == 1:
-            for part in range(2):
+            for part in range(PARTS):
                 arrived(x_one(0, 1 - y, part), xrsem.at[OY + part])
             low_arrived(0)
             project(0)
@@ -425,6 +433,8 @@
             ys_s[zz] = part_s[zz, 1 - y, SQ:, :].astype(BF16)
             send(ys_s.at[zz], yr_s.at[zz], TO_SUM_Y, yrsem.at[zz], ctx=ypeer)
 
+    LR, LL = 7 * PARTS, 7 * PARTS + 3
+
     def top_step(d, s, last, part, out_s, in_s, kind, base, step):
         value = part_s[near(d), :, PART * part : PART * (part + 1), :]
         if s:
@@ -438,12 +448,12 @@
                 send(out_s.at[s, part, yy], in_s.at[s, part, y], kind, ersem.at[base + s], ctx=at_chip(step, yy))
 
     def top_right(s):
-        for part in range(2):
+        for part in range(PARTS):
             top_step(4 - s, s, 3, part, h1rs, h1rr, TO_TR, 4 * part, 1)
 
     def top_left(s):
-        for part in range(2):
-            top_step(s - 3, s, 2, part, h1ls, h1lr, TO_TL, 8 + 3 * part, -1)
+        for part in range(PARTS):
+            top_step(s - 3, s, 2, part, h1ls, h1lr, TO_TL, 4 * PARTS + 3 * part, -1)
 
     def low_value(d):
         arrived(yr_s.at[near(d)], yrsem.at[near(d)])
@@ -452,59 +462,62 @@
     def low_right(s):
         value = low_value(3 - s)
         if s:
-            arrived(h2rr.at[s - 1], ersem.at[13 + s])
+            arrived(h2rr.at[s - 1], ersem.at[LR + s - 1])
             value = value + h2rr[s - 1].astype(F32)
         h2rs[s] = value.astype(BF16)
-        send(h2rs.at[s], h2rr.at[s], TO_LR, ersem.at[14 + s], ctx=right)
+        send(h2rs.at[s], h2rr.at[s], TO_LR, ersem.at[LR + s], ctx=right)
 
     def low_left(s):
         if s == 0:
             h2fs[...] = part_s[near(4), :, SQ:, :].astype(BF16)
             for yy in (y, 1 - y):
-                send(h2fs.at[yy], h2fr.at[y], TO_LF, ersem.at[17], ctx=at_chip(-1, yy))
+                send(h2fs.at[yy], h2fr.at[y], TO_LF, ersem.at[LL], ctx=at_chip(-1, yy))
             return
         value = low_value(s - 4)
         if s == 1:
-            arrived(h2fr, ersem.at[17])
+            arrived(h2fr, ersem.at[LL])
             value = value + (h2fr[0].astype(F32) + h2fr[1].astype(F32))
         else:
-            arrived(h2lr.at[s - 2], ersem.at[16 + s])
+            arrived(h2lr.at[s - 2], ersem.at[LL + s - 1])
             value = value + h2lr[s - 2].astype(F32)
         h2ls[s - 1] = value.astype(BF16)
-        send(h2ls.at[s - 1], h2lr.at[s - 1], TO_LL, ersem.at[17 + s], ctx=left)
+        send(h2ls.at[s - 1], h2lr.at[s - 1], TO_LL, ersem.at[LL + s], ctx=left)
 
     expand(4)
     top_right(0)
     low_left(0)
+    expand(3)
     expand(-3)
     top_left(0)
-    for d in (3, -2, 2, -1, 1, 0):
+    for d in (-2, 2, -1, 1):
         expand(d)
     for s in range(1, 4):
         top_right(s)
+        low_right(s - 1)
         low_left(s)
         if s < 3:
             top_left(s)
-        low_right(s - 1)
+        if s == 2:
+            expand(0)
     arrived(f1r, rsem.at[9])
     top_sum = part_s[z, y, :SQ, :] + f1r[...].astype(F32)
     ends = []
-    for part in range(2):
+    for part in range(PARTS):
         end = top_sum[PART * part : PART * (part + 1)]
         arrived(h1rr.at[3, part], ersem.at[4 * part + 3])
-        arrived(h1lr.at[2, part], ersem.at[8 + 3 * part + 2])
+        arrived(h1lr.at[2, part], ersem.at[4 * PARTS + 3 * part + 2])
         for yy in range(2):
             end = end + (h1rr[3, part, yy].astype(F32) + h1lr[2, part, yy].astype(F32))
         ends.append(end)
     low_sum = low_value(0)
-    arrived(h2rr.at[2], ersem.at[16])
-    arrived(h2lr.at[2], ersem.at[20])
+    arrived(h2rr.at[2], ersem.at[LR + 2])
+    arrived(h2lr.at[2], ersem.at[LL + 3])
     low_sum = low_sum + (h2rr[2].astype(F32) + h2lr[2].astype(F32))
     summed = (jnp.concatenate([*ends, low_sum], axis=0) * w_slot).astype(BF16)
 
-    os_s[...] = dot(summed, take_sib).astype(BF16)
+    os_s[...] = dot(summed, take_s[1]).astype(BF16)
     push(os_s, or_s, ssem.at[10], rsem.at[10], ctx=sib)
-    own_cols = dot(summed, take_own).astype(BF16)
+    own_cols = dot(summed, take_s[0]).astype(BF16)
     arrived(or_s, rsem.at[10])
     o_s[core] = own_cols
     o_s[1 - core] = or_s[...]
@@ -518,7 +531,7 @@
         to = (e + d) % EN
         send(ts_s.at[to], tr_s.at[e], TO_TOK, prsem.at[2], ex=to)
     arrived(rr_s, rsem.at[8])
-    resid = jnp.where(core == e // 4, resid_own, rr_s[...].astype(F32))
+    resid = jnp.where(core == e // 4, ro_s[...], rr_s[...].astype(F32))
     mixed = town_s[e]
     arrived(tr_s.at[pl.ds(0, EN - 1)], prsem.at[2])
     for d in range(1, EN):
@@ -560,13 +573,13 @@
         buf(SH, WIDE), buf(SH, WIDE), buf(ZN, 2, SH, WIDE),
         buf(2, 2, SH, FF, dtype=F32), buf(SH, 128, dtype=F32), buf(ZN, 2, SH, WIDE, dtype=F32),
         buf(ZN, SQ, WIDE), buf(ZN, SQ, WIDE),
-        buf(4, 2, 2, SQ // 2, WIDE), buf(4, 2, 2, SQ // 2, WIDE), buf(3, 2, 2, SQ // 2, WIDE), buf(3, 2, 2, SQ // 2, WIDE),
+        buf(4, PARTS, 2, PART, WIDE), buf(4, PARTS, 2, PART, WIDE), buf(3, PARTS, 2, PART, WIDE), buf(3, PARTS, 2, PART, WIDE),
         buf(3, SQ, WIDE), buf(3, SQ, WIDE), buf(3, SQ, WIDE), buf(3, SQ, WIDE),
         buf(2, SQ, WIDE), buf(2, SQ, WIDE), buf(SQ, WIDE), buf(SQ, WIDE),
-        buf(2, SH, 256), buf(SH, 256), buf(SH, 256), buf(OUTR, 256), buf(OUTR, 256),
+        buf(2, SH, 256), buf(SH, 256), buf(SH, 256), buf(2, SH, HALF), buf(2, WIDE, 256), buf(OUTR, 256, dtype=F32), buf(OUTR, 256), buf(OUTR, 256),
         buf(EN, PACK, HD), buf(EN, PACK, HD), buf(EN, PACK, HD, dtype=F32), buf(Q, SLOTS),
         dma((11,)), dma((11,)), dma((11,)), dma((17,)), dma((4,)), dma((ZN,)), dma((1,)), dma((CHIPS,)),
-        dma((3,)), dma((ZN,)), dma((ZN,)), dma((23,)), dma((21,)),
+        dma((3,)), dma((ZN,)), dma((ZN,)), dma((8 * PARTS + 7,)), dma((7 * PARTS + 7,)),
     ]
     return pl.pallas_call(
         layer_kernel,

time: 91.8 us -> 89.6 us (0.976)
  Pallas kernels: 91.1 us -> 88.9 us
    pallas_call x1, Pallas kernels: 91.1 us -> 88.9 us  [local(): pl.pallas_call(layer_kernel, out_shape=jax.ShapeDtypeStruct((OUTR, COLS),...]
where the time goes in v4:
time: 89.6 us
  Pallas kernels  88.9 us (99%)
    pallas_call x1, Pallas kernels, local(): pl.pallas_call(layer_kernel, out_shape=jax.ShapeDtypeStruct((OUTR, COLS),...  88.9 us

profile of v4, /device:TPU:1, one launch (start us, length us, event | category | flops | bytes accessed | tf_op | source)
XLA Modules:
  0.0 89.6 jit_solution(16790398150129228603)
XLA Ops:
  0.0 88.9 %shard_map.109 = bf16[64,192]{1,0:T(8,128)(2,1)S(1)} custom-call(s32[2,512]{1,0:T(2,128)} %bitcast.8, f32[2,512]{1,0:T(2,128)} %bitcast.9, f32[1,6144]{1,0:T(1,128)} %bitcast.7, bf16[512,768]{1,0:T(8,128)(2,1)} %q_hbm.1, bf16[512,128]{1,0:T(8,128)(2,1)} %k_hbm.1, bf16[512,128]{1,0:T(8,128)(2,1)} %v_hbm.1, bf16[192,512]{1,0:T(8,128)(2,1)} %bitcast.6, ...), custom_call_target="tpu_custom_call" | custom-call | flops 3000000000 | bytes 12000000 | tf_op jit(solution)/shard_map/pallas_call | solution.py:584
  89.0 0.6 copy.13

commit v5 on v4

--- a/solution.py
+++ b/solution.py
@@ -34,6 +34,7 @@
 FF = 256
 PACK = OUTR + OUTR // 2
 MSG = PAIRS + 16
+EXP_FAR = (5, 3, 7, 1, 4, 2, 6)
 GROUP = 4
 PARTS = 2
 PART = SQ // PARTS
@@ -298,7 +299,7 @@
         stream = stream + pr_s[source].astype(F32)
     stream = stream + before_attention
     st_s[e] = stream.astype(BF16)
-    for d in range(1, EN):
+    for d in EXP_FAR:
         to = (e + d) % EN
         send(st_s.at[e], st_s.at[e], TO_EXP_ALL, prsem.at[1], ex=to)
     arrived(st_s.at[pl.ds(0, EN - 1)], prsem.at[1])
@@ -527,7 +528,7 @@
     terms = jnp.concatenate([terms[:, :, :HD], terms[:, :TOKB, HD:] + tails], axis=1)
     town_s[...] = terms
     ts_s[...] = terms.astype(BF16)
-    for d in range(1, EN):
+    for d in EXP_FAR:
         to = (e + d) % EN
         send(ts_s.at[to], tr_s.at[e], TO_TOK, prsem.at[2], ex=to)
     arrived(rr_s, rsem.at[8])

time: 89.6 us -> 88.1 us (0.983)
  Pallas kernels: 88.9 us -> 87.4 us
    pallas_call x1, Pallas kernels: 88.9 us -> 87.4 us  [local(): pl.pallas_call(layer_kernel, out_shape=jax.ShapeDtypeStruct((OUTR, COLS),...]
where the time goes in v5:
time: 88.1 us
  Pallas kernels  87.4 us (99%)
    pallas_call x1, Pallas kernels, local(): pl.pallas_call(layer_kernel, out_shape=jax.ShapeDtypeStruct((OUTR, COLS),...  87.4 us

profile of v5, /device:TPU:1, one launch (start us, length us, event | category | flops | bytes accessed | tf_op | source)
XLA Modules:
  0.0 88.1 jit_solution(6325447035817842127)
XLA Ops:
  0.0 87.4 %shard_map.109 = bf16[64,192]{1,0:T(8,128)(2,1)S(1)} custom-call(s32[2,512]{1,0:T(2,128)} %bitcast.8, f32[2,512]{1,0:T(2,128)} %bitcast.9, f32[1,6144]{1,0:T(1,128)} %bitcast.7, bf16[512,768]{1,0:T(8,128)(2,1)} %q_hbm.1, bf16[512,128]{1,0:T(8,128)(2,1)} %k_hbm.1, bf16[512,128]{1,0:T(8,128)(2,1)} %v_hbm.1, bf16[192,512]{1,0:T(8,128)(2,1)} %bitcast.6, ...), custom_call_target="tpu_custom_call" | custom-call | flops 3000000000 | bytes 12000000 | tf_op jit(solution)/shard_map/pallas_call | solution.py:585
  87.4 0.6 copy.13

commit v6 on v5

--- a/solution.py
+++ b/solution.py
@@ -257,7 +257,7 @@
     arrived(got_s.at[pl.ds(0, ZN - 1)], arsem.at[0])
     att_s[chip] = merge([own_s] + [got_s.at[near(d)] for d in AWAY[:-1]])[0]
     for d in AWAY:
-        for yy in (y, 1 - y):
+        for yy in (1 - y, y):
             if yy is y and d == 0 or yy is not y and d in FAR:
                 continue
             send(att_s.at[chip], att_s.at[chip], TO_CHIPS, brsem.at[chip], ctx=at_chip(d, yy))
@@ -332,7 +332,7 @@
         send(block, block, kind, recv, ctx=to)
 
     def first_hops(part, base, d):
-        for yy in (y, 1 - y):
+        for yy in (1 - y, y):
             same(x_one(0, y, part), TO_FIRST, xrsem.at[base + part], at_chip(d, yy))
 
     same(x_low(0, y), TO_LOW, xrsem.at[LL], left)
@@ -445,7 +445,7 @@
         if s < last:
             send(out_s.at[s, part], in_s.at[s, part], kind, ersem.at[base + s], ctx=at_chip(step, y))
         else:
-            for yy in (y, 1 - y):
+            for yy in (1 - y, y):
                 send(out_s.at[s, part, yy], in_s.at[s, part, y], kind, ersem.at[base + s], ctx=at_chip(step, yy))
 
     def top_right(s):
@@ -471,7 +471,7 @@
     def low_left(s):
         if s == 0:
             h2fs[...] = part_s[near(4), :, SQ:, :].astype(BF16)
-            for yy in (y, 1 - y):
+            for yy in (1 - y, y):
                 send(h2fs.at[yy], h2fr.at[y], TO_LF, ersem.at[LL], ctx=at_chip(-1, yy))
             return
         value = low_value(s - 4)

time: 88.1 us -> 87.8 us (level)
  no operation moved by 1% of the time
where the time goes in v6:
time: 87.8 us; the launch traced here: 87.7 us
  Pallas kernels  87.1 us (99%)
    pallas_call x1, Pallas kernels, local(): pl.pallas_call(layer_kernel, out_shape=jax.ShapeDtypeStruct((OUTR, COLS),...  87.1 us

profile of v6, /device:TPU:1, one launch (start us, length us, event | category | flops | bytes accessed | tf_op | source)
XLA Modules:
  0.0 87.7 jit_solution(11897173981173423179)
XLA Ops:
  0.0 87.1 %shard_map.109 = bf16[64,192]{1,0:T(8,128)(2,1)S(1)} custom-call(s32[2,512]{1,0:T(2,128)} %bitcast.8, f32[2,512]{1,0:T(2,128)} %bitcast.9, f32[1,6144]{1,0:T(1,128)} %bitcast.7, bf16[512,768]{1,0:T(8,128)(2,1)} %q_hbm.1, bf16[512,128]{1,0:T(8,128)(2,1)} %k_hbm.1, bf16[512,128]{1,0:T(8,128)(2,1)} %v_hbm.1, bf16[192,512]{1,0:T(8,128)(2,1)} %bitcast.6, ...), custom_call_target="tpu_custom_call" | custom-call | flops 3000000000 | bytes 12000000 | tf_op jit(solution)/shard_map/pallas_call | solution.py:585
  87.1 0.6 copy.13
